TPU v7x, 128 devices: a whole 4x4x4 slice. The times are simulated.
128 devices in a mesh: band: 8 (over x, y_lo), row: 16 (over z, y_hi, core).
Axes of the slice: x: 4, y: 4 (y_hi: 2, y_lo: 2; y = y_hi * 2 + y_lo), z: 4, core: 2. Of those that a mesh axis runs over, the one named last changes fastest.
Arguments:
- phase: float32 [4096, 4096], P('row'), may hold values from -3.140625 to 3.140625
- aperture: int32 [4096, 4096], P('row'), may hold values 0 or 1
- defocus_index: int32 [16], P('band'), may hold values from 0 to 3
- intensity: float32 [16, 512, 512], P('band', 'row'), may hold values from 0.1 to 3
Outputs:
- gradient: float32 [4096, 4096], P('row', 'band')
All inputs are finite; a program needn't handle non-finite values. No bound on the sum of `aperture` on one device may be relied on, other than what follows from the above.
Results may differ from a plain program's by a relative error of at most 0.0032.
Values may be sent and summed in bfloat16 or wider, within the bound.
No kernel may reach another device: no remote copies, remote signals or barrier semaphores. Data moves between devices by JAX's collectives and lax.ppermute only.
A program may use at most 128 MiB of HBM per device.

v0:
```python
import math

import jax
import jax.numpy as jnp
from jax import lax
from jax.sharding import PartitionSpec as P

defocus_strength = math.pi


def focal_table(wave_index, waves, focal_width, pupil_width):
    scale_ratio = 1.0 / (1.0 + wave_index.astype(jnp.float32) / waves)
    column = 2 * lax.broadcasted_iota(jnp.int32, (focal_width, pupil_width), 1) - pupil_width + 1
    offset = 2 * lax.broadcasted_iota(jnp.int32, (focal_width, pupil_width), 0) - focal_width
    phase_angle = (column * offset).astype(jnp.float32) * (
        scale_ratio * (math.pi / (4.0 * pupil_width))
    )
    normalizer = 1.0 / math.sqrt(pupil_width)
    return jnp.stack(
        [jnp.cos(phase_angle) * normalizer, -jnp.sin(phase_angle) * normalizer]
    ).astype(jnp.bfloat16)


def pupil_field(phase, aperture, defocus_level, first_row, pupil_width):
    row_pos = (
        2 * (first_row + lax.broadcasted_iota(jnp.int32, phase.shape, 0)) - pupil_width + 1
    ).astype(jnp.float32)
    col_pos = (2 * lax.broadcasted_iota(jnp.int32, phase.shape, 1) - pupil_width + 1).astype(
        jnp.float32
    )
    radius = (row_pos * row_pos + col_pos * col_pos) / float(pupil_width * pupil_width)
    shifted = phase + defocus_level.astype(jnp.float32) * defocus_strength * radius
    amplitude = aperture.astype(jnp.float32)
    return (amplitude * jnp.cos(shifted), amplitude * jnp.sin(shifted))


def pupil_products(pupil_pair, table):
    blocks = lax.dot_general(
        pupil_pair, table, (((2,), (2,)), ((), ())), preferred_element_type=jnp.float32
    )
    real_part = blocks[0, :, 0] - blocks[1, :, 1]
    imag_part = blocks[0, :, 1] + blocks[1, :, 0]
    return jnp.stack([real_part, imag_part]).astype(jnp.bfloat16)


def focal_rows(products, table_cols):
    blocks = lax.dot_general(
        products, table_cols, (((1,), (2,)), ((), ())), preferred_element_type=jnp.float32
    )
    real_part = blocks[0, :, 0] - blocks[1, :, 1]
    imag_part = blocks[0, :, 1] + blocks[1, :, 0]
    return jnp.concatenate([real_part, imag_part], axis=1)


def back_rows(weighted, table_cols):
    unit_count = weighted.shape[0]
    table_width = table_cols.shape[1]
    halves = weighted.reshape(unit_count, 2, table_width)
    blocks = lax.dot_general(
        halves, table_cols, (((2,), (1,)), ((), ())), preferred_element_type=jnp.float32
    )
    real_part = blocks[:, 0, 0] + blocks[:, 1, 1]
    imag_part = blocks[:, 1, 0] - blocks[:, 0, 1]
    return jnp.stack([real_part, imag_part]).astype(jnp.bfloat16)


def phase_gradient(back, table, field_re, field_im):
    blocks = lax.dot_general(
        back, table, (((1,), (1,)), ((), ())), preferred_element_type=jnp.float32
    )
    spread_re = blocks[0, :, 0] + blocks[1, :, 1]
    spread_im = blocks[1, :, 0] - blocks[0, :, 1]
    return spread_im * field_re - spread_re * field_im


def local(phase, aperture, defocus_index, intensity):
    row_count = phase.shape[0]
    pupil_width = phase.shape[1]
    local_waves = intensity.shape[0]
    focal_width = intensity.shape[2]
    first_row = lax.axis_index("row") * row_count
    band_start = lax.axis_index("band") * local_waves
    total_waves = local_waves * lax.axis_size("band")
    running = jnp.zeros((row_count, pupil_width), jnp.float32)
    for member in range(local_waves):
        wave_index = band_start + member
        table = focal_table(wave_index, total_waves, focal_width, pupil_width)
        field_re, field_im = pupil_field(
            phase, aperture, defocus_index[member], first_row, pupil_width
        )
        pupil_pair = jnp.stack([field_re, field_im]).astype(jnp.bfloat16)
        products = pupil_products(pupil_pair, table)
        table_cols = lax.dynamic_slice_in_dim(table, first_row, row_count, 2)
        focal = lax.psum_scatter(
            focal_rows(products, table_cols), "row", scatter_dimension=0, tiled=True
        )
        focal_re = focal[:, :focal_width]
        focal_im = focal[:, focal_width:]
        misfit = focal_re * focal_re + focal_im * focal_im - intensity[member]
        weighted = jnp.concatenate([misfit * focal_re, misfit * focal_im], axis=1).astype(
            jnp.bfloat16
        )
        back = back_rows(lax.all_gather(weighted, "row", axis=0, tiled=True), table_cols)
        gradient = phase_gradient(back, table, field_re, field_im)
        running = running + gradient
    return lax.psum_scatter(running, "band", scatter_dimension=1, tiled=True)


def solution(mesh):
    return jax.shard_map(
        local,
        mesh=mesh,
        in_specs=(P("row", None), P("row", None), P("band"), P("band", "row", None)),
        out_specs=P("row", "band"),
        check_vma=False,
    )
```

profile of v0, /device:TPU:1, one launch (start us, length us, event | category | flops | bytes accessed | tf_op | source)
XLA Modules:
  0.0 509.1 jit_solution(2497417982271974181)
XLA Ops:
  6.7 1.3 fusion.75
  9.3 0.0 copy-start.8
  9.3 0.0 copy-start.10
  9.3 62.6 %multiply_convert_fusion.3 = (bf16[1,512,4096]{2,1,0:T(8,128)(2,1)}, bf16[1,512,4096]{2,1,0:T(8,128)(2,1)S(1)}, bf16[1,512,4096]{2,1,0:T(8,128)(2,1)S(1)}, bf16[1,512,4096]{2,1,0:T(8,128)(2,1)}) fusion(f32[]{:T(128)S(6)} %mul.229, s32[512]{0:T(512)S(1)} %multiply_add_fusion.1, s32[4096]{0:T(1024)S(1)} %multiply_add_fusion, f32[]{:T(128)S(6)} %mul.246), kind=kLoop, calls=%fused_computation.11 | loop fusion | flops 29360128 | bytes 16795656 | tf_op jit(solution)/shard_map/convert.26
  71.9 0.0 copy-done.8
  71.9 0.0 copy-done.10
  71.9 31.9 %convert_bitcast_fusion.3 = (bf16[1,256,4096]{2,1,0:T(8,128)(2,1)}, bf16[1,256,4096]{2,1,0:T(8,128)(2,1)}, bf16[1,256,4096]{2,1,0:T(8,128)(2,1)S(1)}, bf16[1,256,4096]{2,1,0:T(8,128)(2,1)S(1)}) fusion(f32[256,4096]{1,0:T(8,128)S(1)} %copy-done.8, f32[]{:T(128)} %bitcast, f32[4096]{0:T(1024)S(1)} %convert_multiply_fusion.2, ...), kind=kLoop, calls=%fused_computation.52 | loop fusion | flops 14680064 | bytes 16794632 | tf_op jit(solution)/shard_map/stack | solution.py:91
  103.8 4.5 fusion.8
  108.3 0.2 fusion.61
  108.5 1.7 fusion.46
  110.3 0.5 fusion.28
  110.7 0.2 pad_maximum_fusion.3
  110.9 1.9 copy.59
  112.8 0.0 reduce-scatter.12.cloned.1.call-update
  112.8 0.0 reduce-scatter.10.cloned.1.call-start
  112.9 9.3 %fusion.4 = f32[2,256,2,512]{3,1,2,0:T(8,128)S(1)} fusion(bf16[1,512,4096]{2,1,0:T(8,128)(2,1)} %get-tuple-element.30, bf16[1,512,4096]{2,1,0:T(8,128)(2,1)} %get-tuple-element.27, bf16[1,256,4096]{2,1,0:T(8,128)(2,1)} %get-tuple-element.6, bf16[1,256,4096]{2,1,0:T(8,128)(2,1)} %get-tuple-element.5), kind=kOutput, calls=%fused_computation.17 | convolution fusion | flops 4320133120 | bytes 14680064 | tf_op jit(solution)/shard_map/dot_general | solution.py:38
  122.2 0.2 fusion.57
  122.4 0.7 fusion.41
  123.1 0.5 fusion.30
  123.6 0.2 pad_maximum_fusion.2
  123.8 0.0 copy-start.12
  123.8 1.8 copy.57
  125.6 0.0 reduce-scatter.10.cloned.1.call-update
  125.6 0.0 all-gather.5.cloned.1.call-start
  125.7 59.7 %reduce-scatter.12.cloned.1.call-done = f32[32,1024]{1,0:T(8,128)} async-done(((f32[512,1024]{1,0:T(8,128)}), f32[32,1024]{1,0:T(8,128)}) %reduce-scatter.12.cloned.1.call-update) | async-done | bytes 131088 | tf_op jit(solution)/shard_map/reduce_scatter | solution.py:94
  185.4 74.5 %reduce-scatter.10.cloned.1.call-done = f32[32,1024]{1,0:T(8,128)} async-done(((f32[512,1024]{1,0:T(8,128)}), f32[32,1024]{1,0:T(8,128)}) %reduce-scatter.10.cloned.1.call-update) | async-done | bytes 131088 | tf_op jit(solution)/shard_map/reduce_scatter | solution.py:94
  259.9 1.0 multiply_convert_fusion.7
  260.9 0.6 pad_maximum_fusion.5
  261.5 0.0 all-gather.5.cloned.1.call-update
  261.5 0.0 all-gather.3.cloned.1.call-start
  261.6 0.6 pad_maximum_fusion.4
  262.2 0.0 all-gather.3.cloned.1.call-update
  262.2 0.0 reduce-scatter.8.cloned.1.call-start
  262.3 46.4 %all-gather.5.cloned.1.call-done = bf16[512,1024]{1,0:T(8,128)(2,1)} async-done(((bf16[32,1024]{1,0:T(8,128)(2,1)}), bf16[512,1024]{1,0:T(8,128)(2,1)}) %all-gather.5.cloned.1.call-update) | async-done | bytes 1048592 | tf_op jit(solution)/shard_map/all_gather | solution.py:103
  308.7 1.5 copy.38
  310.2 1.8 fusion.51
  312.0 0.1 fusion.63
  312.1 42.6 %all-gather.3.cloned.1.call-done = bf16[512,1024]{1,0:T(8,128)(2,1)} async-done(((bf16[32,1024]{1,0:T(8,128)(2,1)}), bf16[512,1024]{1,0:T(8,128)(2,1)}) %all-gather.3.cloned.1.call-update) | async-done | bytes 1048592 | tf_op jit(solution)/shard_map/all_gather | solution.py:103
  354.7 1.5 copy.33
  356.2 1.9 fusion.54
  358.1 0.1 fusion.59
  358.2 0.3 copy-done.5
  358.5 1.3 copy-done.7
  359.8 8.2 %fusion.2 = f32[2,256,2,4096]{3,1,2,0:T(8,128)} fusion(bf16[1,512,4096]{2,1,0:T(8,128)(2,1)S(1)} %copy-done.7, bf16[1,512,4096]{2,1,0:T(8,128)(2,1)S(1)} %copy-done.5, bf16[1,512,256]{2,1,0:T(8,128)(2,1)S(1)} %get-tuple-element.14, bf16[1,512,256]{2,1,0:T(8,128)(2,1)S(1)} %get-tuple-element.13), kind=kOutput, calls=%fused_computation.16 | convolution fusion | flops 4312793088 | bytes 25690112 | tf_op jit(solution)/shard_map/dot_general | solution.py:68
  368.0 8.2 %fusion.6 = f32[2,256,2,4096]{3,1,2,0:T(8,128)} fusion(bf16[1,512,4096]{2,1,0:T(8,128)(2,1)S(1)} %copy-done.3, bf16[1,512,4096]{2,1,0:T(8,128)(2,1)S(1)} %copy-done.1, bf16[1,512,256]{2,1,0:T(8,128)(2,1)S(1)} %get-tuple-element.18, bf16[1,512,256]{2,1,0:T(8,128)(2,1)S(1)} %get-tuple-element.17), kind=kOutput, calls=%fused_computation.18 | convolution fusion | flops 4312793088 | bytes 25690112 | tf_op jit(solution)/shard_map/dot_general | solution.py:68
  376.1 37.7 %fusion.15 = f32[256,4096]{1,0:T(8,128)} fusion(f32[2,256,2,4096]{3,1,2,0:T(8,128)} %fusion.6, f32[2,256,2,4096]{3,1,2,0:T(8,128)} %fusion.2, f32[256,4096]{1,0:T(8,128)S(1)} %copy-done.9, f32[]{:T(128)} %bitcast, f32[4096]{0:T(1024)S(1)} %convert_multiply_fusion.2, f32[256]{0:T(256)S(1)} %convert_multiply_fusion.3, s32[256,4096]{1,0:T(8,128)S(1)} %copy-done.11, ...), kind=kLoop, calls=%fused_computation.26 | loop fusion | flops 22020096 | bytes 46154760 | tf_op jit(solution)/shard_map/add | solution.py:105
  413.9 0.0 reduce-scatter.8.cloned.1.call-update
  413.9 88.6 %reduce-scatter.8.cloned.1.call-done = f32[256,512]{1,0:T(8,128)} async-done(((f32[256,4096]{1,0:T(8,128)}), f32[256,512]{1,0:T(8,128)}) %reduce-scatter.8.cloned.1.call-update) | async-done | bytes 524304 | tf_op jit(solution)/shard_map/reduce_scatter | solution.py:106
  (24 shorter events, 0.1 us)
Async XLA Ops:
  6.5 178.9 %reduce-scatter.12.cloned.1.call-start = ((), (), s32[]{:S(2)}) async-start(), calls=%async_computation.7 | async-start | bytes 2228224 | tf_op jit(solution)/shard_map/reduce_scatter | solution.py:94
  9.3 62.6 %copy-start.8 = (f32[256,4096]{1,0:T(8,128)S(1)}, f32[256,4096]{1,0:T(8,128)}, u32[]{:S(2)}) copy-start(f32[256,4096]{1,0:T(8,128)} %param.4) | copy-start | bytes 12582916
  9.3 62.6 %copy-start.10 = (s32[256,4096]{1,0:T(8,128)S(1)}, s32[256,4096]{1,0:T(8,128)}, u32[]{:S(2)}) copy-start(s32[256,4096]{1,0:T(8,128)} %param.5) | copy-start | bytes 12582916
  71.9 31.9 %copy-start = (bf16[1,512,4096]{2,1,0:T(8,128)(2,1)}, bf16[1,512,4096]{2,1,0:T(8,128)(2,1)S(1)}, u32[]{:S(2)}) copy-start(bf16[1,512,4096]{2,1,0:T(8,128)(2,1)S(1)} %get-tuple-element.28) | copy-start | bytes 12582916
  71.9 31.9 %copy-start.2 = (bf16[1,512,4096]{2,1,0:T(8,128)(2,1)}, bf16[1,512,4096]{2,1,0:T(8,128)(2,1)S(1)}, u32[]{:S(2)}) copy-start(bf16[1,512,4096]{2,1,0:T(8,128)(2,1)S(1)} %get-tuple-element.29) | copy-start | bytes 12582916
  112.8 147.1 %reduce-scatter.10.cloned.1.call-start = ((), (), s32[]{:S(2)}) async-start(), calls=%async_computation.6 | async-start | bytes 2228224 | tf_op jit(solution)/shard_map/reduce_scatter | solution.py:94
  112.9 9.5 %copy-start.4 = (bf16[1,512,4096]{2,1,0:T(8,128)(2,1)S(1)}, bf16[1,512,4096]{2,1,0:T(8,128)(2,1)}, u32[]{:S(2)}) copy-start(bf16[1,512,4096]{2,1,0:T(8,128)(2,1)} %get-tuple-element.27) | copy-start | bytes 12582916
  112.9 9.5 %copy-start.6 = (bf16[1,512,4096]{2,1,0:T(8,128)(2,1)S(1)}, bf16[1,512,4096]{2,1,0:T(8,128)(2,1)}, u32[]{:S(2)}) copy-start(bf16[1,512,4096]{2,1,0:T(8,128)(2,1)} %get-tuple-element.30) | copy-start | bytes 12582916
  123.8 136.1 %copy-start.12 = (f32[2,32,512]{2,1,0:T(8,128)S(1)}, f32[2,32,512]{2,1,0:T(8,128)}, u32[]{:S(2)}) copy-start(f32[2,32,512]{2,1,0:T(8,128)} %param.7) | copy-start | bytes 393220
  125.6 183.0 %all-gather.5.cloned.1.call-start = ((), (), s32[]{:S(2)}) async-start(), calls=%async_computation.4 | async-start | bytes 1114112 | tf_op jit(solution)/shard_map/all_gather | solution.py:103
  261.5 93.1 %all-gather.3.cloned.1.call-start = ((), (), s32[]{:S(2)}) async-start(), calls=%async_computation.3 | async-start | bytes 1114112 | tf_op jit(solution)/shard_map/all_gather | solution.py:103
  262.2 240.3 %reduce-scatter.8.cloned.1.call-start = ((), (), s32[]{:S(2)}) async-start(), calls=%async_computation.5 | async-start | bytes 4718592 | tf_op jit(solution)/shard_map/reduce_scatter | solution.py:106
  356.2 2.4 copy-start.5
  356.2 3.6 copy-start.7
  359.8 8.2 %copy-start.1 = (bf16[1,512,4096]{2,1,0:T(8,128)(2,1)S(1)}, bf16[1,512,4096]{2,1,0:T(8,128)(2,1)}, u32[]{:S(2)}) copy-start(bf16[1,512,4096]{2,1,0:T(8,128)(2,1)} %copy-done) | copy-start | bytes 12582916
  359.8 8.2 %copy-start.3 = (bf16[1,512,4096]{2,1,0:T(8,128)(2,1)S(1)}, bf16[1,512,4096]{2,1,0:T(8,128)(2,1)}, u32[]{:S(2)}) copy-start(bf16[1,512,4096]{2,1,0:T(8,128)(2,1)} %copy-done.2) | copy-start | bytes 12582916
  368.0 8.2 %copy-start.9 = (f32[256,4096]{1,0:T(8,128)S(1)}, f32[256,4096]{1,0:T(8,128)}, u32[]{:S(2)}) copy-start(f32[256,4096]{1,0:T(8,128)} %param.4) | copy-start | bytes 12582916
  368.0 8.2 %copy-start.11 = (s32[256,4096]{1,0:T(8,128)S(1)}, s32[256,4096]{1,0:T(8,128)}, u32[]{:S(2)}) copy-start(s32[256,4096]{1,0:T(8,128)} %param.5) | copy-start | bytes 12582916
Sparse Core Ops, SparseCore 0:
  112.9 72.4 reduce-scatter.11
  189.8 70.0 reduce-scatter.9
  262.4 46.2 all-gather.4
  311.0 43.6 all-gather.2
  414.0 88.4 reduce-scatter.7
where the time goes:
time: 509 us
  waiting for transfers between devices  312 us (61%)
  other arithmetic  136 us (27%)
  matrix products  36.3 us (7%)
  between operations  14.7 us (3%)
  local copies, waits for them, and re-layouts  9.65 us (2%)
    reduce_scatter x2, waiting for transfers between devices, local(): lax.psum_scatter(focal_rows(products, table_cols), 'row', scatter_dimensi...  134 us
    all_gather x2, waiting for transfers between devices, local(): lax.all_gather(weighted, 'row', axis=0, tiled=True)  89 us
    reduce_scatter x1, waiting for transfers between devices, local(): return lax.psum_scatter(running, 'band', scatter_dimension=1, tiled=True)  88.6 us
    another operation x2, other arithmetic  63.5 us
    add x1, other arithmetic, local(): running = running + gradient  37.7 us
    another operation x1, other arithmetic, local(): pupil_pair = jnp.stack([field_re, field_im]).astype(jnp.bfloat16)  31.9 us
    dot_general x2, matrix products, phase_gradient(): lax.dot_general(back, table, (((1,), (1,)), ((), ())), preferred_element_...  16.3 us
    dot_general x2, matrix products, pupil_products(): lax.dot_general(pupil_pair, table, (((2,), (2,)), ((), ())), preferred_el...  13.8 us
  transfers between devices with their start and end apart: 5, of which 5 were waited for; matrix products, arithmetic and copies ran while one was open for 3% of the time, Pallas kernels for 0%

commit v1 on v0

v1 whole, which is shorter than its diff:
```python
import math

import jax
import jax.numpy as jnp
from jax import lax
from jax.experimental import pallas as pl
from jax.experimental.pallas import tpu as pltpu
from jax.sharding import PartitionSpec as P

F32 = jnp.float32
BF16 = jnp.bfloat16
N = 4096
M = 512
HALF = N // 2
K = M // 2
ROWS = 256
BLK = 256
STEPS = HALF // BLK
WL = 2
GRP = 32
NORM = 1.0 / math.sqrt(N)

SIN_C = (9.99999246e-01, -1.66656827e-01, 8.31325871e-03, -1.85243573e-04)
COS_C = (9.99999953e-01, -4.99999053e-01, 4.16635847e-02, -1.38537043e-03, 2.31539316e-05)
SIN_T = (6.28318492, -41.34159016, 81.5999729, -76.61480386, 41.34439753, -12.47366849)
COS_T = (0.99999999, -19.73920453, 64.93911898, -85.45016555, 60.16783172, -25.96831326, 6.52961036)


def poly(coefs, y):
    acc = coefs[-1]
    for c in coefs[-2::-1]:
        acc = acc * y + c
    return acc


def turn(t):
    t = t - jnp.floor(t + 0.5)
    y = t * t
    return poly(COS_T, y), t * poly(SIN_T, y)


def unit(phi):
    y = phi * phi
    r2 = math.sqrt(2.0)
    c = poly([r2 * v / 4.0**n for n, v in enumerate(COS_C)], y)
    s = phi * poly([0.5 * r2 * v / 4.0**n for n, v in enumerate(SIN_C)], y)
    return c, s


def field(phi, amp):
    c, s = unit(phi)
    a_s = amp * s
    return amp - s * a_s, a_s * c


def lane_rev(x):
    rows, lanes = x.shape
    idx = 127 - lax.broadcasted_iota(jnp.int32, (rows, 128), 1)
    parts = [
        jnp.take_along_axis(x[:, s : s + 128], idx, axis=1, mode="promise_in_bounds")
        for s in range(lanes - 128, -1, -128)
    ]
    return jnp.concatenate(parts, axis=1) if len(parts) > 1 else parts[0]


def nt(a, b):
    return lax.dot_general(a, b, (((1,), (1,)), ((), ())), preferred_element_type=F32)


def nn(a, b):
    return lax.dot_general(a, b, (((1,), (0,)), ((), ())), preferred_element_type=F32)


def span(meta, w):
    return (1024 * (16 + meta[1] + w)).astype(F32)


def angle(n, m):
    inv = 1.0 / m
    q = jnp.floor(n * inv + 0.5)
    return turn((n - q * m) * inv)


def chirp_cols(meta, w, first, lanes):
    x = (2 * (first + lax.broadcasted_iota(jnp.int32, (1, lanes), 1)) + 1).astype(F32)
    return turn(x * x * (meta[2 + w].astype(F32) * (0.5 / (N * N))))


def chirp_rows(meta, w, row_pos):
    x = (2 * row_pos - (N - 1)).astype(F32)
    return turn(x * x * (meta[2 + w].astype(F32) * (0.5 / (N * N))))


def flip_matrix(flip):
    r = lax.broadcasted_iota(jnp.int32, (ROWS, ROWS), 0)
    c = lax.broadcasted_iota(jnp.int32, (ROWS, ROWS), 1)
    return jnp.where(jnp.where(flip, ROWS - 1 - c, c) == r, 1.0, 0.0).astype(BF16)


def forward_kernel(meta, ph_r, ph_l, ap_r, ap_l, tab, fld, out, z, rot, e_s, o_s, xacc, yacc, tmp):
    i = pl.program_id(0)

    @pl.when(i == 0)
    def _():
        xacc[...] = jnp.zeros_like(xacc)
        yacc[...] = jnp.zeros_like(yacc)
        for w in range(WL):
            m = span(meta, w)

            def init(t, _):
                r0 = pl.multiple_of(t * 32, 32)
                k = lax.broadcasted_iota(jnp.int32, (32, BLK), 0) + (r0 + 1)
                j = 2 * lax.broadcasted_iota(jnp.int32, (32, BLK), 1) + 1
                c, s = angle((k * j).astype(F32), m)
                z[w, 0, pl.ds(r0, 32), :] = c * NORM
                z[w, 1, pl.ds(r0, 32), :] = s * NORM
                k = lax.broadcasted_iota(jnp.int32, (32, 128), 0) + (r0 + 1)
                c, s = angle((k * (2 * BLK)).astype(F32), m)
                rot[w, 0, pl.ds(r0, 32), :] = c
                rot[w, 1, pl.ds(r0, 32), :] = s
                return 0

            lax.fori_loop(0, 8, init, 0)

    @pl.when(i > 0)
    def _():
        for w in range(WL):

            def step(t, _):
                r0 = pl.multiple_of(t * 32, 32)
                rc, rs = rot[w, 0, pl.ds(r0, 32), :], rot[w, 1, pl.ds(r0, 32), :]
                for h in (0, 128):
                    zc = z[w, 0, pl.ds(r0, 32), h : h + 128]
                    zs = z[w, 1, pl.ds(r0, 32), h : h + 128]
                    z[w, 0, pl.ds(r0, 32), h : h + 128] = zc * rc - zs * rs
                    z[w, 1, pl.ds(r0, 32), h : h + 128] = zc * rs + zs * rc
                return 0

            lax.fori_loop(0, 8, step, 0)

    dx = [chirp_cols(meta, w, i * BLK, BLK) for w in range(WL)]

    def rows(t, _):
        r0 = pl.multiple_of(t * 32, 32)
        sl = pl.ds(r0, 32)
        fr_c, fr_s = field(ph_r[sl, :], ap_r[sl, :].astype(F32))
        fl_c, fl_s = field(lane_rev(ph_l[sl, :]), lane_rev(ap_l[sl, :].astype(F32)))
        fld[0, sl, :] = fr_c
        fld[1, sl, :] = fr_s
        fld[2, sl, :] = fl_c
        fld[3, sl, :] = fl_s
        ec, es = fr_c + fl_c, fr_s + fl_s
        oc, os = fr_c - fl_c, fr_s - fl_s
        for w in range(WL):
            dc, ds = dx[w]
            e_s[w, 0, sl, :] = (ec * dc - es * ds).astype(BF16)
            e_s[w, 1, sl, :] = (ec * ds + es * dc).astype(BF16)
            o_s[w, 0, sl, :] = (oc * dc - os * ds).astype(BF16)
            o_s[w, 1, sl, :] = (oc * ds + os * dc).astype(BF16)
        return 0

    lax.fori_loop(0, ROWS // 32, rows, 0)
    ones = jnp.full((16, BLK), NORM, BF16)
    for w in range(WL):
        c = z[w, 0].astype(BF16)
        s = z[w, 1].astype(BF16)
        tab[w, 0] = c
        tab[w, 1] = s
        c = jnp.concatenate([c, ones], axis=0)
        for part in range(2):
            xacc[w, part] += nt(c, e_s[w, part])
            yacc[w, part] += nt(s, o_s[w, part])

    @pl.when(i == STEPS - 1)
    def _():
        row0 = meta[0] * ROWS
        j = flip_matrix(meta[0] < 8)
        pos = row0 + lax.broadcasted_iota(jnp.int32, (1, ROWS), 1)
        for w in range(WL):
            dc, ds = chirp_rows(meta, w, pos)
            xr, xi = xacc[w, 0], xacc[w, 1]
            yr, yi = yacc[w, 0], yacc[w, 1]
            xr, xi = xr * dc - xi * ds, xr * ds + xi * dc
            yr, yi = yr * dc - yi * ds, yr * ds + yi * dc
            x0 = (xr[K : K + 1], xi[K : K + 1])
            xr, xi = xr[:K], xi[:K]
            plus = (xr + yi, xi - yr)
            minus = (xr - yi, xi + yr)
            for part in range(2):
                tmp[pl.ds(8, K), :] = plus[part]
                tmp[pl.ds(7, 1), :] = x0[part]
                p = nn(tmp[pl.ds(7, K), :].astype(BF16), j).astype(BF16)
                m = nn(minus[part].astype(BF16), j).astype(BF16)
                at = (w * 2 + part) * GRP
                for g in range(8):
                    out[8 + g, at : at + GRP, :] = p[g * GRP : (g + 1) * GRP]
                    out[7 - g, at : at + GRP, :] = m[g * GRP : (g + 1) * GRP]


def focal_kernel(x, tab, obs, out):
    last = lax.broadcasted_iota(jnp.int32, (GRP, K), 1) == K - 1
    for w in range(WL):
        at = w * 2 * GRP
        acc_c = jnp.zeros((2 * GRP, K), F32)
        acc_s = jnp.zeros((2 * GRP, K), F32)
        centre = jnp.zeros((2 * GRP, BLK), F32)
        for i in range(STEPS):
            r = x[8 + i, at : at + 2 * GRP, :].astype(F32)
            l = x[7 - i, at : at + 2 * GRP, :].astype(F32)
            e = r + l
            centre = centre + e
            cols = slice(i * BLK, (i + 1) * BLK)
            acc_c = acc_c + nt(e.astype(BF16), tab[w, 0, :, cols])
            acc_s = acc_s + nt((r - l).astype(BF16), tab[w, 1, :, cols])
        centre = jnp.sum(centre, axis=1, keepdims=True) * NORM
        cr, ci = acc_c[:GRP], acc_c[GRP:]
        sr, si = acc_s[:GRP], acc_s[GRP:]
        weighted = []
        for side, (fr, fi) in enumerate(
            (
                (jnp.where(last, centre[:GRP], cr + si), jnp.where(last, centre[GRP:], ci - sr)),
                (cr - si, ci + sr),
            )
        ):
            misfit = fr * fr + fi * fi - obs[w, :, side * K : (side + 1) * K]
            weighted.append(
                [(misfit * fr).astype(BF16).astype(F32), (misfit * fi).astype(BF16).astype(F32)]
            )
        (pr, pi), (mr, mi) = weighted
        centre = jnp.concatenate([pr[:, K - 1 :], pi[:, K - 1 :]], axis=0) * NORM
        p = jnp.concatenate([jnp.where(last, 0.0, pr), jnp.where(last, 0.0, pi)], axis=0)
        m = jnp.concatenate([mr, mi], axis=0)
        s = (p + m).astype(BF16)
        d = (p - m).astype(BF16)
        for i in range(STEPS):
            cols = slice(i * BLK, (i + 1) * BLK)
            bc = nn(s, tab[w, 0, :, cols]) + centre
            bs = nn(d, tab[w, 1, :, cols])
            bcr, bci, bsr, bsi = bc[:GRP], bc[GRP:], bs[:GRP], bs[GRP:]
            out[8 + i, at : at + GRP, :] = (bcr - bsi).astype(BF16)
            out[8 + i, at + GRP : at + 2 * GRP, :] = (bci + bsr).astype(BF16)
            out[7 - i, at : at + GRP, :] = (bcr + bsi).astype(BF16)
            out[7 - i, at + GRP : at + 2 * GRP, :] = (bci - bsr).astype(BF16)


def gradient_kernel(meta, x, tab, fld, out, lhs, mid, sp, tmp):
    i = pl.program_id(0)

    @pl.when(i == 0)
    def _():
        flip = meta[0] < 8
        j = flip_matrix(flip)
        lane = lax.broadcasted_iota(jnp.int32, (1, ROWS), 1)
        pos = meta[0] * ROWS + jnp.where(flip, ROWS - 1 - lane, lane)
        for w in range(WL):
            dc, ds = chirp_rows(meta, w, pos)
            p, m, b0 = [], [], []
            for part in range(2):
                at = (w * 2 + part) * GRP
                for g in range(8):
                    tmp[g * GRP : (g + 1) * GRP, :] = x[8 + g, at : at + GRP, :].astype(F32)
                tmp[K : K + 8, :] = jnp.zeros((8, ROWS), F32)
                b0.append(tmp[0:1, :])
                p.append(tmp[pl.ds(1, K), :])
                m.append(
                    jnp.concatenate([x[7 - g, at : at + GRP, :] for g in range(8)], axis=0).astype(F32)
                )
            for n, (re, im) in enumerate(
                ((p[0] + m[0], p[1] + m[1]), (p[0] - m[0], p[1] - m[1]))
            ):
                lhs[w, 2 * n] = nt(j, (re * dc + im * ds).astype(BF16)).astype(BF16)
                lhs[w, 2 * n + 1] = nt(j, (im * dc - re * ds).astype(BF16)).astype(BF16)
            for part, v in enumerate((b0[0] * dc + b0[1] * ds, b0[1] * dc - b0[0] * ds)):
                v = jnp.broadcast_to((v * NORM).astype(BF16), (128, ROWS))
                mid[w, part] = nt(j, v)

    for w in range(WL):
        c = tab[w, 0]
        s = tab[w, 1]
        for part in range(2):
            sp[w, part] = nn(lhs[w, part], c)
            sp[w, 2 + part] = nn(lhs[w, 2 + part], s)
    dx = [chirp_cols(meta, w, i * BLK, BLK) for w in range(WL)]
    right = 4 + i // 2, pl.multiple_of((i % 2) * BLK, BLK)
    left = 3 - i // 2, pl.multiple_of((1 - i % 2) * BLK, BLK)

    def rows(t, _):
        r0 = pl.multiple_of(t * 32, 32)
        sl = pl.ds(r0, 32)
        tot = [0.0, 0.0, 0.0, 0.0]
        for w in range(WL):
            dc, ds = dx[w]
            m = [jnp.concatenate([mid[w, part, sl, :]] * 2, axis=1) for part in range(2)]
            cr, ci = sp[w, 0, sl, :] + m[0], sp[w, 1, sl, :] + m[1]
            sr, si = sp[w, 2, sl, :], sp[w, 3, sl, :]
            tot[0] += cr * dc + ci * ds
            tot[1] += ci * dc - cr * ds
            tot[2] += sr * dc + si * ds
            tot[3] += si * dc - sr * ds
        cr, ci, sr, si = tot
        g_r = (ci + sr) * fld[0, sl, :] - (cr - si) * fld[1, sl, :]
        g_l = (ci - sr) * fld[2, sl, :] - (cr + si) * fld[3, sl, :]
        out[right[0], sl, pl.ds(right[1], BLK)] = g_r.astype(BF16)
        out[left[0], sl, pl.ds(left[1], BLK)] = lane_rev(g_l).astype(BF16)
        return 0

    lax.fori_loop(0, ROWS // 32, rows, 0)


def run_forward(meta, phase, aperture):
    smem = pl.BlockSpec(memory_space=pltpu.SMEM)
    right = pl.BlockSpec((ROWS, BLK), lambda i: (0, STEPS + i))
    left = pl.BlockSpec((ROWS, BLK), lambda i: (0, STEPS - 1 - i))
    return pl.pallas_call(
        forward_kernel,
        grid=(STEPS,),
        out_shape=(
            jax.ShapeDtypeStruct((WL, 2, K, HALF), BF16),
            jax.ShapeDtypeStruct((4, ROWS, HALF), F32),
            jax.ShapeDtypeStruct((16, WL * 2 * GRP, ROWS), BF16),
        ),
        in_specs=[smem, right, left, right, left],
        out_specs=(
            pl.BlockSpec((WL, 2, K, BLK), lambda i: (0, 0, 0, i)),
            pl.BlockSpec((4, ROWS, BLK), lambda i: (0, 0, i)),
            pl.BlockSpec((16, WL * 2 * GRP, ROWS), lambda i: (0, 0, 0)),
        ),
        scratch_shapes=[
            pltpu.VMEM((WL, 2, K, BLK), F32),
            pltpu.VMEM((WL, 2, K, 128), F32),
            pltpu.VMEM((WL, 2, ROWS, BLK), BF16),
            pltpu.VMEM((WL, 2, ROWS, BLK), BF16),
            pltpu.VMEM((WL, 2, K + 16, ROWS), F32),
            pltpu.VMEM((WL, 2, K, ROWS), F32),
            pltpu.VMEM((K + 16, ROWS), F32),
        ],
        compiler_params=pltpu.CompilerParams(vmem_limit_bytes=40 * 2**20),
        name="forward",
    )(meta, phase, phase, aperture, aperture)


def run_focal(x, tab, obs):
    return pl.pallas_call(
        focal_kernel,
        out_shape=jax.ShapeDtypeStruct((16, WL * 2 * GRP, ROWS), BF16),
        in_specs=[pl.BlockSpec(memory_space=pltpu.VMEM)] * 3,
        out_specs=pl.BlockSpec(memory_space=pltpu.VMEM),
        compiler_params=pltpu.CompilerParams(vmem_limit_bytes=32 * 2**20),
        name="focal",
    )(x, tab, obs)


def run_gradient(meta, x, tab, fld):
    return pl.pallas_call(
        gradient_kernel,
        grid=(STEPS,),
        out_shape=jax.ShapeDtypeStruct((8, ROWS, M), BF16),
        in_specs=[
            pl.BlockSpec(memory_space=pltpu.SMEM),
            pl.BlockSpec((16, WL * 2 * GRP, ROWS), lambda i: (0, 0, 0)),
            pl.BlockSpec((WL, 2, K, BLK), lambda i: (0, 0, 0, i)),
            pl.BlockSpec((4, ROWS, BLK), lambda i: (0, 0, i)),
        ],
        out_specs=pl.BlockSpec((8, ROWS, M), lambda i: (0, 0, 0)),
        scratch_shapes=[
            pltpu.VMEM((WL, 4, ROWS, K), BF16),
            pltpu.VMEM((WL, 2, ROWS, 128), F32),
            pltpu.VMEM((WL, 4, ROWS, BLK), F32),
            pltpu.VMEM((K + 8, ROWS), F32),
        ],
        compiler_params=pltpu.CompilerParams(vmem_limit_bytes=40 * 2**20),
        name="gradient",
    )(meta, x, tab, fld)


def fold(intensity, row):
    turned = jnp.where(row < 8, jnp.flip(intensity, axis=1), intensity)
    return jnp.concatenate(
        [turned[:, :, K + 1 :], turned[:, :, K : K + 1], jnp.flip(turned[:, :, :K], axis=2)], axis=2
    )


def local(phase, aperture, defocus_index, intensity):
    row = lax.axis_index("row")
    band = lax.axis_index("band")
    meta = jnp.concatenate(
        [jnp.stack([row, band * WL]).astype(jnp.int32), defocus_index.astype(jnp.int32)]
    )
    obs = fold(intensity, row)
    tab, fld, sent = run_forward(meta, phase, aperture)
    got = lax.all_to_all(sent, "row", 0, 0, tiled=True)
    sent = run_focal(got, tab, obs)
    got = lax.all_to_all(sent, "row", 0, 0, tiled=True)
    parts = run_gradient(meta, got, tab, fld)
    parts = lax.all_to_all(parts, "band", 0, 0, tiled=True)
    return jnp.sum(parts.astype(F32), axis=0)


def solution(mesh):
    return jax.shard_map(
        local,
        mesh=mesh,
        in_specs=(P("row", None), P("row", None), P("band"), P("band", "row", None)),
        out_specs=P("row", "band"),
        check_vma=False,
    )
```

time: 509 us -> 125 us (0.25)
  waiting for transfers between devices: 312 us -> 16.7 us
  other arithmetic: 136 us -> 1.94 us
  blocking collectives: 0 us -> 49.2 us
  Pallas kernels: 0 us -> 36.9 us
  matrix products: 36.3 us -> 0 us
  between operations: 14.7 us -> 0.06 us
  starting transfers between devices: 0.17 us -> 9.46 us
    reduce_scatter x3 -> x0, waiting for transfers between devices: 223 us -> none  [the longest x2 134 us: local(): lax.psum_scatter(focal_rows(products, table_cols), 'row', scatter_dimensi...]
    another operation x3 -> x0, other arithmetic: 95.4 us -> none
    all_gather x2 -> x0, waiting for transfers between devices: 89 us -> none  [local(): lax.all_gather(weighted, 'row', axis=0, tiled=True)]
    all_to_all x0 -> x2, blocking collectives: none -> 49.2 us  [the longest x1 28.8 us: local(): parts = lax.all_to_all(parts, 'band', 0, 0, tiled=True)]
    add x4 -> x0, other arithmetic: 38 us -> none  [the longest x1 37.7 us: local(): running = running + gradient]
    pallas_call x0 -> x3, Pallas kernels: none -> 36.9 us  [the longest x1 20.2 us: run_forward(): pl.pallas_call(forward_kernel, grid=(STEPS,), out_shape=(jax.ShapeDtypeSt...]
    dot_general x8 -> x0, matrix products: 36.3 us -> none  [the longest x2 16.3 us: phase_gradient(): lax.dot_general(back, table, (((1,), (1,)), ((), ())), preferred_element_...]
    all_to_all x0 -> x1, waiting for transfers between devices: none -> 16.7 us  [local(): got = lax.all_to_all(sent, 'row', 0, 0, tiled=True)]
  transfers between devices with their start and end apart: 5 -> 1, of which waited for: 5 -> 1; matrix products, arithmetic and copies ran while one was open for 3% -> 0% of each run, Pallas kernels for 0% -> 0%
where the time goes in v1:
time: 125 us; the launch traced here: 123 us
  blocking collectives  49.2 us (39%)
  Pallas kernels  36.9 us (30%)
  waiting for transfers between devices  16.7 us (13%)
  starting transfers between devices  9.46 us (8%)
  local copies, waits for them, and re-layouts  8.91 us (7%)
  other arithmetic  1.94 us (2%)
    all_to_all x1, blocking collectives, local(): parts = lax.all_to_all(parts, 'band', 0, 0, tiled=True)  28.8 us
    all_to_all x1, blocking collectives, local(): got = lax.all_to_all(sent, 'row', 0, 0, tiled=True)  20.4 us
    pallas_call x1, Pallas kernels, run_forward(): pl.pallas_call(forward_kernel, grid=(STEPS,), out_shape=(jax.ShapeDtypeSt...  20.2 us
    all_to_all x1, waiting for transfers between devices, local(): got = lax.all_to_all(sent, 'row', 0, 0, tiled=True)  16.7 us
    pallas_call x1, Pallas kernels, run_gradient(): pl.pallas_call(gradient_kernel, grid=(STEPS,), out_shape=jax.ShapeDtypeSt...  14.3 us
    all_to_all x1, starting transfers between devices, local(): got = lax.all_to_all(sent, 'row', 0, 0, tiled=True)  9.46 us
    unnamed x12, local copies, waits for them, and re-layouts  8.54 us
  transfers between devices with their start and end apart: 1, of which 1 were waited for; matrix products, arithmetic and copies ran while one was open for 0% of the time, Pallas kernels for 0%

profile of v1, /device:TPU:1, one launch (start us, length us, event | category | flops | bytes accessed | tf_op | source)
XLA Modules:
  0.0 123.1 jit_solution(7416324901241904208)
XLA Ops:
  0.0 0.7 pad_add_fusion.meta
  0.7 0.0 copy-start
  0.7 2.2 %copy-done = f32[256,4096]{1,0:T(8,128)S(1)} copy-done((f32[256,4096]{1,0:T(8,128)S(1)}, f32[256,4096]{1,0:T(8,128)}, u32[]{:S(2)}) %copy-start) | copy-done | bytes 4194328
  2.9 0.0 copy-start.1
  2.9 2.2 %copy-done.1 = s32[256,4096]{1,0:T(8,128)S(1)} copy-done((s32[256,4096]{1,0:T(8,128)S(1)}, s32[256,4096]{1,0:T(8,128)}, u32[]{:S(2)}) %copy-start.1) | copy-done | bytes 4194328
  5.1 0.0 copy-start.5
  5.1 20.2 %forward.1 = (bf16[2,2,256,2048]{3,2,1,0:T(8,128)(2,1)S(1)}, f32[4,256,2048]{2,1,0:T(8,128)}, bf16[16,128,256]{2,1,0:T(8,128)(2,1)}) custom-call(s32[4]{0:T(128)S(1)} %pad_add_fusion.meta, f32[256,4096]{1,0:T(8,128)S(1)} %copy-done, f32[256,4096]{1,0:T(8,128)S(1)} %copy-done, s32[256,4096]{1,0:T(8,128)S(1)} %copy-done.1, s32[256,4096]{1,0:T(8,128)S(1)} %copy-done.1), custom_call_target="tpu_custom_call" | custom-call | tf_op jit(solution)/shard_map/forward/pallas_call | solution.py:314
  25.3 0.0 copy-start.2
  25.3 2.0 %copy-done.2 = bf16[2,2,256,2048]{3,2,1,0:T(8,128)(2,1)} copy-done((bf16[2,2,256,2048]{3,2,1,0:T(8,128)(2,1)}, bf16[2,2,256,2048]{3,2,1,0:T(8,128)(2,1)S(1)}, u32[]{:S(2)}) %copy-start.2) | copy-done | bytes 4194328
  27.3 9.5 %all-to-all-start = ((bf16[16,128,256]{2,1,0:T(8,128)(2,1)}), bf16[16,128,256]{2,1,0:T(8,128)(2,1)S(1)}, u32[]{:S(2)}, u32[]{:S(2)}) async-start(bf16[16,128,256]{2,1,0:T(8,128)(2,1)} %get-tuple-element.8), calls=%async_computation | async-start | bytes 2097152 | tf_op jit(solution)/shard_map/all_to_all | solution.py:391
  36.8 0.0 copy-done.5
  36.8 0.1 rev.8
  36.9 0.1 slice.12
  37.0 0.2 rev.9
  37.2 0.1 pad_maximum_fusion.obs
  37.3 16.7 %all-to-all-done.x = bf16[16,128,256]{2,1,0:T(8,128)(2,1)S(1)} async-done(((bf16[16,128,256]{2,1,0:T(8,128)(2,1)}), bf16[16,128,256]{2,1,0:T(8,128)(2,1)S(1)}, u32[]{:S(2)}, u32[]{:S(2)}) %all-to-all-start) | async-done | bytes 1048608 | tf_op jit(solution)/shard_map/all_to_all | solution.py:391
  54.0 0.0 copy-start.3
  54.0 2.2 %copy-done.3 = bf16[2,2,256,2048]{3,2,1,0:T(8,128)(2,1)S(1)} copy-done((bf16[2,2,256,2048]{3,2,1,0:T(8,128)(2,1)S(1)}, bf16[2,2,256,2048]{3,2,1,0:T(8,128)(2,1)}, u32[]{:S(2)}) %copy-start.3) | copy-done | bytes 4194328
  56.1 0.0 copy-start.4
  56.2 2.4 %focal.1 = bf16[16,128,256]{2,1,0:T(8,128)(2,1)S(1)} custom-call(bf16[16,128,256]{2,1,0:T(8,128)(2,1)S(1)} %all-to-all-done.x, bf16[2,2,256,2048]{3,2,1,0:T(8,128)(2,1)S(1)} %copy-done.3, f32[2,32,512]{2,1,0:T(8,128)S(1)} %pad_maximum_fusion.obs), custom_call_target="tpu_custom_call" | custom-call | tf_op jit(solution)/shard_map/focal/pallas_call | solution.py:343
  58.6 20.4 %all_to_all.15.x = bf16[16,128,256]{2,1,0:T(8,128)(2,1)S(1)} all-to-all(bf16[16,128,256]{2,1,0:T(8,128)(2,1)S(1)} %focal.1), channel_id=1, replica_groups=mesh['band'=8,'row'=16] {'row'}, dimensions={0} | all-to-all | bytes 2097152 | tf_op jit(solution)/shard_map/all_to_all | solution.py:393
  78.9 0.0 copy-done.4
  78.9 14.3 %gradient.1 = bf16[8,256,512]{2,1,0:T(8,128)(2,1)S(1)} custom-call(s32[4]{0:T(128)S(1)} %pad_add_fusion.meta, bf16[16,128,256]{2,1,0:T(8,128)(2,1)S(1)} %all_to_all.15.x, bf16[2,2,256,2048]{3,2,1,0:T(8,128)(2,1)S(1)} %copy-done.4, f32[4,256,2048]{2,1,0:T(8,128)} %get-tuple-element.10.fld), custom_call_target="tpu_custom_call" | custom-call | tf_op jit(solution)/shard_map/gradient/pallas_call | solution.py:354
  93.2 28.8 %all_to_all.16 = bf16[8,256,512]{2,1,0:T(8,128)(2,1)S(1)} all-to-all(bf16[8,256,512]{2,1,0:T(8,128)(2,1)S(1)} %gradient.1), channel_id=1, replica_groups=mesh['band'=8,'row'=16] {'band'}, dimensions={0} | all-to-all | bytes 4194304 | tf_op jit(solution)/shard_map/all_to_all | solution.py:395
  122.0 1.1 convert_reduce_fusion
  (3 shorter events, 0.0 us)
Async XLA Ops:
  0.7 2.2 %copy-start = (f32[256,4096]{1,0:T(8,128)S(1)}, f32[256,4096]{1,0:T(8,128)}, u32[]{:S(2)}) copy-start(f32[256,4096]{1,0:T(8,128)} %ph_l.1) | copy-start | bytes 12582916
  2.9 2.2 %copy-start.1 = (s32[256,4096]{1,0:T(8,128)S(1)}, s32[256,4096]{1,0:T(8,128)}, u32[]{:S(2)}) copy-start(s32[256,4096]{1,0:T(8,128)} %ap_l.1) | copy-start | bytes 12582916
  5.1 31.6 %copy-start.5 = (f32[2,32,512]{2,1,0:T(8,128)S(1)}, f32[2,32,512]{2,1,0:T(8,128)}, u32[]{:S(2)}) copy-start(f32[2,32,512]{2,1,0:T(8,128)} %param.7) | copy-start | bytes 393220
  25.3 2.0 %copy-start.2 = (bf16[2,2,256,2048]{3,2,1,0:T(8,128)(2,1)}, bf16[2,2,256,2048]{3,2,1,0:T(8,128)(2,1)S(1)}, u32[]{:S(2)}) copy-start(bf16[2,2,256,2048]{3,2,1,0:T(8,128)(2,1)S(1)} %get-tuple-element.9.tab) | copy-start | bytes 12582916
  27.3 26.7 %all-to-all-start = ((bf16[16,128,256]{2,1,0:T(8,128)(2,1)}), bf16[16,128,256]{2,1,0:T(8,128)(2,1)S(1)}, u32[]{:S(2)}, u32[]{:S(2)}) async-start(bf16[16,128,256]{2,1,0:T(8,128)(2,1)} %get-tuple-element.8), calls=%async_computation | async-start | bytes 2097152 | tf_op jit(solution)/shard_map/all_to_all | solution.py:391
  54.0 2.2 %copy-start.3 = (bf16[2,2,256,2048]{3,2,1,0:T(8,128)(2,1)S(1)}, bf16[2,2,256,2048]{3,2,1,0:T(8,128)(2,1)}, u32[]{:S(2)}) copy-start(bf16[2,2,256,2048]{3,2,1,0:T(8,128)(2,1)} %copy-done.2) | copy-start | bytes 12582916
  56.1 22.8 %copy-start.4 = (bf16[2,2,256,2048]{3,2,1,0:T(8,128)(2,1)S(1)}, bf16[2,2,256,2048]{3,2,1,0:T(8,128)(2,1)}, u32[]{:S(2)}) copy-start(bf16[2,2,256,2048]{3,2,1,0:T(8,128)(2,1)} %copy-done.2) | copy-start | bytes 12582916

commit v2 on v1

--- a/solution.py
+++ b/solution.py
@@ -334,7 +334,7 @@
             pltpu.VMEM((WL, 2, K, ROWS), F32),
             pltpu.VMEM((K + 16, ROWS), F32),
         ],
-        compiler_params=pltpu.CompilerParams(vmem_limit_bytes=40 * 2**20),
+        compiler_params=pltpu.CompilerParams(vmem_limit_bytes=60 * 2**20),
         name="forward",
     )(meta, phase, phase, aperture, aperture)
 
@@ -345,7 +345,7 @@
         out_shape=jax.ShapeDtypeStruct((16, WL * 2 * GRP, ROWS), BF16),
         in_specs=[pl.BlockSpec(memory_space=pltpu.VMEM)] * 3,
         out_specs=pl.BlockSpec(memory_space=pltpu.VMEM),
-        compiler_params=pltpu.CompilerParams(vmem_limit_bytes=32 * 2**20),
+        compiler_params=pltpu.CompilerParams(vmem_limit_bytes=60 * 2**20),
         name="focal",
     )(x, tab, obs)
 
@@ -368,7 +368,7 @@
             pltpu.VMEM((WL, 4, ROWS, BLK), F32),
             pltpu.VMEM((K + 8, ROWS), F32),
         ],
-        compiler_params=pltpu.CompilerParams(vmem_limit_bytes=40 * 2**20),
+        compiler_params=pltpu.CompilerParams(vmem_limit_bytes=60 * 2**20),
         name="gradient",
     )(meta, x, tab, fld)
 
@@ -386,7 +386,7 @@
     meta = jnp.concatenate(
         [jnp.stack([row, band * WL]).astype(jnp.int32), defocus_index.astype(jnp.int32)]
     )
-    obs = fold(intensity, row)
+    obs, meta = lax.optimization_barrier((fold(intensity, row), meta))
     tab, fld, sent = run_forward(meta, phase, aperture)
     got = lax.all_to_all(sent, "row", 0, 0, tiled=True)
     sent = run_focal(got, tab, obs)

time: 125 us -> 127 us (1.016)
  blocking collectives: 49.2 us -> 78.7 us
  waiting for transfers between devices: 16.7 us -> 0 us
  starting transfers between devices: 9.46 us -> 0 us
  local copies, waits for them, and re-layouts: 8.91 us -> 1.8 us
  Pallas kernels: 36.9 us -> 41.8 us
    all_to_all x1 -> x2, blocking collectives: 20.4 us -> 49.7 us  [local(): got = lax.all_to_all(sent, 'row', 0, 0, tiled=True)]
    all_to_all x1 -> x0, waiting for transfers between devices: 16.7 us -> none  [local(): got = lax.all_to_all(sent, 'row', 0, 0, tiled=True)]
    all_to_all x1 -> x0, starting transfers between devices: 9.46 us -> none  [local(): got = lax.all_to_all(sent, 'row', 0, 0, tiled=True)]
    unnamed x12 -> x0, local copies, waits for them, and re-layouts: 8.54 us -> none
    pallas_call x1, Pallas kernels: 2.4 us -> 5.93 us  [run_focal(): pl.pallas_call(focal_kernel, out_shape=jax.ShapeDtypeStruct((16, WL * 2 *...]
    rev x1, local copies, waits for them, and re-layouts: 0.11 us -> 1.54 us  [fold(): turned = jnp.where(row < 8, jnp.flip(intensity, axis=1), intensity)]
    pallas_call x1, Pallas kernels: 14.3 us -> 15.6 us  [run_gradient(): pl.pallas_call(gradient_kernel, grid=(STEPS,), out_shape=jax.ShapeDtypeSt...]
  transfers between devices with their start and end apart: 1 -> 0, of which waited for: 1 -> 0; matrix products, arithmetic and copies ran while one was open for 0% -> 0% of each run, Pallas kernels for 0% -> 0%
where the time goes in v2:
time: 127 us; the launch traced here: 125 us
  blocking collectives  78.7 us (62%)
  Pallas kernels  41.8 us (33%)
  other arithmetic  3.14 us (2%)
  local copies, waits for them, and re-layouts  1.8 us (1%)
    all_to_all x2, blocking collectives, local(): got = lax.all_to_all(sent, 'row', 0, 0, tiled=True)  49.7 us
    all_to_all x1, blocking collectives, local(): parts = lax.all_to_all(parts, 'band', 0, 0, tiled=True)  29 us
    pallas_call x1, Pallas kernels, run_forward(): pl.pallas_call(forward_kernel, grid=(STEPS,), out_shape=(jax.ShapeDtypeSt...  20.2 us
    pallas_call x1, Pallas kernels, run_gradient(): pl.pallas_call(gradient_kernel, grid=(STEPS,), out_shape=jax.ShapeDtypeSt...  15.6 us
    pallas_call x1, Pallas kernels, run_focal(): pl.pallas_call(focal_kernel, out_shape=jax.ShapeDtypeStruct((16, WL * 2 *...  5.93 us

profile of v2, /device:TPU:1, one launch (start us, length us, event | category | flops | bytes accessed | tf_op | source)
XLA Modules:
  0.0 125.4 jit_solution(15985337816124122732)
XLA Ops:
  0.0 1.5 %rev.8 = f32[2,32,512]{2,1,0:T(8,128)S(1)} reverse(f32[2,32,512]{2,1,0:T(8,128)} %param.7), dimensions={1} | reverse | bytes 262144 | tf_op jit(solution)/shard_map/jit(_flip)/rev | solution.py:377
  1.6 0.1 slice.12
  1.7 0.2 rev.9
  1.8 1.3 %pad_add_fusion.meta = s32[4]{0:T(128)} fusion(s32[2]{0:T(128)} %param.6, s32[1]{0:T(128)} %bitcast.1, s32[1]{0:T(128)} %bitcast), kind=kLoop, calls=%fused_computation.3 | loop fusion | flops 8 | bytes 32 | tf_op jit(solution)/shard_map/concatenate | solution.py:386
  3.1 0.7 pad_maximum_fusion.obs
  3.9 20.2 %forward.1 = (bf16[2,2,256,2048]{3,2,1,0:T(8,128)(2,1)}, f32[4,256,2048]{2,1,0:T(8,128)}, bf16[16,128,256]{2,1,0:T(8,128)(2,1)}) custom-call(s32[4]{0:T(128)} %pad_add_fusion.meta, f32[256,4096]{1,0:T(8,128)} %ph_l.1, f32[256,4096]{1,0:T(8,128)} %ph_l.1, s32[256,4096]{1,0:T(8,128)} %ap_l.1, s32[256,4096]{1,0:T(8,128)} %ap_l.1), custom_call_target="tpu_custom_call" | custom-call | tf_op jit(solution)/shard_map/forward/pallas_call | solution.py:314
  24.1 27.4 %all_to_all.15.x = bf16[16,128,256]{2,1,0:T(8,128)(2,1)} all-to-all(bf16[16,128,256]{2,1,0:T(8,128)(2,1)} %get-tuple-element.11), channel_id=1, replica_groups=mesh['band'=8,'row'=16] {'row'}, dimensions={0} | all-to-all | bytes 2097152 | tf_op jit(solution)/shard_map/all_to_all | solution.py:391
  51.5 5.9 %focal.1 = bf16[16,128,256]{2,1,0:T(8,128)(2,1)} custom-call(bf16[16,128,256]{2,1,0:T(8,128)(2,1)} %all_to_all.15.x, bf16[2,2,256,2048]{3,2,1,0:T(8,128)(2,1)} %get-tuple-element.12.tab, f32[2,32,512]{2,1,0:T(8,128)} %pad_maximum_fusion.obs), custom_call_target="tpu_custom_call" | custom-call | tf_op jit(solution)/shard_map/focal/pallas_call | solution.py:343
  57.4 22.3 %all_to_all.16.x = bf16[16,128,256]{2,1,0:T(8,128)(2,1)} all-to-all(bf16[16,128,256]{2,1,0:T(8,128)(2,1)} %focal.1), channel_id=1, replica_groups=mesh['band'=8,'row'=16] {'row'}, dimensions={0} | all-to-all | bytes 2097152 | tf_op jit(solution)/shard_map/all_to_all | solution.py:393
  79.7 15.6 %gradient.1 = bf16[8,256,512]{2,1,0:T(8,128)(2,1)} custom-call(s32[4]{0:T(128)} %pad_add_fusion.meta, bf16[16,128,256]{2,1,0:T(8,128)(2,1)} %all_to_all.16.x, bf16[2,2,256,2048]{3,2,1,0:T(8,128)(2,1)} %get-tuple-element.12.tab, f32[4,256,2048]{2,1,0:T(8,128)} %get-tuple-element.14.fld), custom_call_target="tpu_custom_call" | custom-call | tf_op jit(solution)/shard_map/gradient/pallas_call | solution.py:354
  95.3 29.0 %all_to_all.17 = bf16[8,256,512]{2,1,0:T(8,128)(2,1)S(1)} all-to-all(bf16[8,256,512]{2,1,0:T(8,128)(2,1)} %gradient.1), channel_id=1, replica_groups=mesh['band'=8,'row'=16] {'band'}, dimensions={0} | all-to-all | bytes 4194304 | tf_op jit(solution)/shard_map/all_to_all | solution.py:395
  124.3 1.1 convert_reduce_fusion
  (3 shorter events, 0.0 us)

commit v3 on v2

v3 whole, which is shorter than its diff:
```python
import math

import jax
import jax.numpy as jnp
from jax import lax
from jax.experimental import pallas as pl
from jax.experimental.pallas import tpu as pltpu
from jax.sharding import PartitionSpec as P

F32 = jnp.float32
BF16 = jnp.bfloat16
N = 4096
M = 512
HALF = N // 2
K = M // 2
ROWS = 256
BLK = 256
CB = 512
SUB = 256
CHUNK = 32
STEPS = HALF // BLK
WL = 2
GRP = 32
NORM = 1.0 / math.sqrt(N)

SIN_C = (9.99999246e-01, -1.66656827e-01, 8.31325871e-03, -1.85243573e-04)
COS_C = (9.99999953e-01, -4.99999053e-01, 4.16635847e-02, -1.38537043e-03, 2.31539316e-05)
SIN_T = (6.28318492, -41.34159016, 81.5999729, -76.61480386, 41.34439753, -12.47366849)
COS_T = (0.99999999, -19.73920453, 64.93911898, -85.45016555, 60.16783172, -25.96831326, 6.52961036)


def poly(coefs, y):
    acc = coefs[-1]
    for c in coefs[-2::-1]:
        acc = acc * y + c
    return acc


def turn(t):
    t = t - jnp.floor(t + 0.5)
    y = t * t
    return poly(COS_T, y), t * poly(SIN_T, y)


def unit(phi):
    y = phi * phi
    r2 = math.sqrt(2.0)
    c = poly([r2 * v / 4.0**n for n, v in enumerate(COS_C)], y)
    s = phi * poly([0.5 * r2 * v / 4.0**n for n, v in enumerate(SIN_C)], y)
    return c, s


def field(phi, amp):
    c, s = unit(phi)
    a_s = amp * s
    return amp - s * a_s, a_s * c


def lane_rev(x):
    rows, lanes = x.shape
    idx = 127 - lax.broadcasted_iota(jnp.int32, (rows, 128), 1)
    parts = [
        jnp.take_along_axis(x[:, s : s + 128], idx, axis=1, mode="promise_in_bounds")
        for s in range(lanes - 128, -1, -128)
    ]
    return jnp.concatenate(parts, axis=1) if len(parts) > 1 else parts[0]


def nt(a, b):
    return lax.dot_general(a, b, (((1,), (1,)), ((), ())), preferred_element_type=F32)


def nn(a, b):
    return lax.dot_general(a, b, (((1,), (0,)), ((), ())), preferred_element_type=F32)


def span(w):
    return (1024 * (16 + lax.axis_index("band") * WL + w)).astype(F32)


def angle(n, m):
    inv = 1.0 / m
    q = jnp.floor(n * inv + 0.5)
    return turn((n - q * m) * inv)


def chirp_cols(level, first, lanes):
    x = (2 * (first + lax.broadcasted_iota(jnp.int32, (1, lanes), 1)) + 1).astype(F32)
    return turn(x * x * (level.astype(F32) * (0.5 / (N * N))))


def chirp_rows(level, row_pos):
    x = (2 * row_pos - (N - 1)).astype(F32)
    return turn(x * x * (level.astype(F32) * (0.5 / (N * N))))


def flip_matrix(flip):
    r = lax.broadcasted_iota(jnp.int32, (ROWS, ROWS), 0)
    c = lax.broadcasted_iota(jnp.int32, (ROWS, ROWS), 1)
    return jnp.where(jnp.where(flip, ROWS - 1 - c, c) == r, 1.0, 0.0).astype(BF16)


def write_tables(tab, first):
    k = lax.broadcasted_iota(jnp.int32, (8, 128), 0) + 1
    lane = lax.broadcasted_iota(jnp.int32, (8, 128), 1)
    at, state = [], []
    for w in range(WL):
        m = span(w)
        for t in range(0, CB, 128):
            x = 2 * (first + t + lane) + 1
            c, s = angle((x * k).astype(F32), m)
            rc, rs = angle((x * 8).astype(F32), m)
            at.append((w, t))
            state.append((c * NORM, s * NORM, rc, rs))
    for q in range(K // 16):
        for n, (w, t) in enumerate(at):
            c0, s0, rc, rs = state[n]
            c1, s1 = c0 * rc - s0 * rs, c0 * rs + s0 * rc
            rows, lanes = slice(16 * q, 16 * q + 16), slice(t, t + 128)
            tab[w, 0, rows, lanes] = jnp.concatenate([c0, c1], axis=0).astype(BF16)
            tab[w, 1, rows, lanes] = jnp.concatenate([s0, s1], axis=0).astype(BF16)
            state[n] = (c1 * rc - s1 * rs, c1 * rs + s1 * rc, rc, rs)


def forward_kernel(level, ph_r, ph_l, ap_r, ap_l, tab, fld, out, e_s, o_s, xacc, yacc, tmp):
    i = pl.program_id(0)
    row = lax.axis_index("row")

    @pl.when(i == 0)
    def _():
        xacc[...] = jnp.zeros_like(xacc)
        yacc[...] = jnp.zeros_like(yacc)

    write_tables(tab, i * CB)
    dx = [chirp_cols(level[w], i * CB, CB) for w in range(WL)]
    ones = jnp.full((16, SUB), NORM, BF16)
    for h in range(0, CB, SUB):
        cols = slice(h, h + SUB)
        mirror = slice(CB - SUB - h, CB - h)
        for r0 in range(0, ROWS, CHUNK):
            sl = slice(r0, r0 + CHUNK)
            fr_c, fr_s = field(ph_r[sl, cols], ap_r[sl, cols].astype(F32))
            fl_c, fl_s = field(lane_rev(ph_l[sl, mirror]), lane_rev(ap_l[sl, mirror]).astype(F32))
            fld[0, sl, cols] = fr_c
            fld[1, sl, cols] = fr_s
            fld[2, sl, cols] = fl_c
            fld[3, sl, cols] = fl_s
            ec, es = fr_c + fl_c, fr_s + fl_s
            oc, os = fr_c - fl_c, fr_s - fl_s
            for w in range(WL):
                dc, ds = dx[w][0][:, cols], dx[w][1][:, cols]
                e_s[w, 0, sl, cols] = (ec * dc - es * ds).astype(BF16)
                e_s[w, 1, sl, cols] = (ec * ds + es * dc).astype(BF16)
                o_s[w, 0, sl, cols] = (oc * dc - os * ds).astype(BF16)
                o_s[w, 1, sl, cols] = (oc * ds + os * dc).astype(BF16)
        for w in range(WL):
            c = jnp.concatenate([tab[w, 0, :, cols], ones], axis=0)
            s = tab[w, 1, :, cols]
            for part in range(2):
                xacc[w, part] += nt(c, e_s[w, part, :, cols])
                yacc[w, part] += nt(s, o_s[w, part, :, cols])

    @pl.when(i == HALF // CB - 1)
    def _():
        j = flip_matrix(row < 8)
        pos = row * ROWS + lax.broadcasted_iota(jnp.int32, (1, ROWS), 1)
        for w in range(WL):
            dc, ds = chirp_rows(level[w], pos)
            xr, xi = xacc[w, 0], xacc[w, 1]
            yr, yi = yacc[w, 0], yacc[w, 1]
            xr, xi = xr * dc - xi * ds, xr * ds + xi * dc
            yr, yi = yr * dc - yi * ds, yr * ds + yi * dc
            x0 = (xr[K : K + 1], xi[K : K + 1])
            xr, xi = xr[:K], xi[:K]
            plus = (xr + yi, xi - yr)
            minus = (xr - yi, xi + yr)
            for part in range(2):
                tmp[pl.ds(8, K), :] = plus[part]
                tmp[pl.ds(7, 1), :] = x0[part]
                p = nn(tmp[pl.ds(7, K), :].astype(BF16), j).astype(BF16)
                m = nn(minus[part].astype(BF16), j).astype(BF16)
                at = (w * 2 + part) * GRP
                for g in range(8):
                    out[8 + g, at : at + GRP, :] = p[g * GRP : (g + 1) * GRP]
                    out[7 - g, at : at + GRP, :] = m[g * GRP : (g + 1) * GRP]


def focal_kernel(x, tab, seen, out, obs):
    low = lax.axis_index("row") < 8
    for w in range(WL):
        for r in range(GRP):
            obs[w, pl.ds(jnp.where(low, GRP - 1 - r, r), 1), :] = seen[w, r : r + 1, :]
    last = lax.broadcasted_iota(jnp.int32, (GRP, K), 1) == K - 1
    for w in range(WL):
        at = w * 2 * GRP
        acc_c = jnp.zeros((2 * GRP, K), F32)
        acc_s = jnp.zeros((2 * GRP, K), F32)
        centre = jnp.zeros((2 * GRP, BLK), F32)
        for i in range(STEPS):
            r = x[8 + i, at : at + 2 * GRP, :].astype(F32)
            l = x[7 - i, at : at + 2 * GRP, :].astype(F32)
            e = r + l
            centre = centre + e
            cols = slice(i * BLK, (i + 1) * BLK)
            acc_c = acc_c + nt(e.astype(BF16), tab[w, 0, :, cols])
            acc_s = acc_s + nt((r - l).astype(BF16), tab[w, 1, :, cols])
        centre = jnp.sum(centre, axis=1, keepdims=True) * NORM
        cr, ci = acc_c[:GRP], acc_c[GRP:]
        sr, si = acc_s[:GRP], acc_s[GRP:]
        rest = pltpu.roll(obs[w, :, K:], K - 1, 1)
        weighted = []
        for side, (fr, fi) in enumerate(
            (
                (jnp.where(last, centre[:GRP], cr + si), jnp.where(last, centre[GRP:], ci - sr)),
                (cr - si, ci + sr),
            )
        ):
            misfit = fr * fr + fi * fi - (rest if side == 0 else lane_rev(obs[w, :, :K]))
            weighted.append(
                [(misfit * fr).astype(BF16).astype(F32), (misfit * fi).astype(BF16).astype(F32)]
            )
        (pr, pi), (mr, mi) = weighted
        centre = jnp.concatenate([pr[:, K - 1 :], pi[:, K - 1 :]], axis=0) * NORM
        p = jnp.concatenate([jnp.where(last, 0.0, pr), jnp.where(last, 0.0, pi)], axis=0)
        m = jnp.concatenate([mr, mi], axis=0)
        s = (p + m).astype(BF16)
        d = (p - m).astype(BF16)
        for i in range(STEPS):
            cols = slice(i * BLK, (i + 1) * BLK)
            bc = nn(s, tab[w, 0, :, cols]) + centre
            bs = nn(d, tab[w, 1, :, cols])
            bcr, bci, bsr, bsi = bc[:GRP], bc[GRP:], bs[:GRP], bs[GRP:]
            out[8 + i, at : at + GRP, :] = (bcr - bsi).astype(BF16)
            out[8 + i, at + GRP : at + 2 * GRP, :] = (bci + bsr).astype(BF16)
            out[7 - i, at : at + GRP, :] = (bcr + bsi).astype(BF16)
            out[7 - i, at + GRP : at + 2 * GRP, :] = (bci - bsr).astype(BF16)


def gradient_kernel(level, x, tab, fld, out, lhs, mid, sp, tmp):
    i = pl.program_id(0)
    row = lax.axis_index("row")

    @pl.when(i == 0)
    def _():
        flip = row < 8
        j = flip_matrix(flip)
        lane = lax.broadcasted_iota(jnp.int32, (1, ROWS), 1)
        pos = row * ROWS + jnp.where(flip, ROWS - 1 - lane, lane)
        for w in range(WL):
            dc, ds = chirp_rows(level[w], pos)
            p, m, b0 = [], [], []
            for part in range(2):
                at = (w * 2 + part) * GRP
                for g in range(8):
                    tmp[g * GRP : (g + 1) * GRP, :] = x[8 + g, at : at + GRP, :].astype(F32)
                tmp[K : K + 8, :] = jnp.zeros((8, ROWS), F32)
                b0.append(tmp[0:1, :])
                p.append(tmp[pl.ds(1, K), :])
                m.append(
                    jnp.concatenate([x[7 - g, at : at + GRP, :] for g in range(8)], axis=0).astype(F32)
                )
            for n, (re, im) in enumerate(
                ((p[0] + m[0], p[1] + m[1]), (p[0] - m[0], p[1] - m[1]))
            ):
                lhs[w, 2 * n] = nt(j, (re * dc + im * ds).astype(BF16)).astype(BF16)
                lhs[w, 2 * n + 1] = nt(j, (im * dc - re * ds).astype(BF16)).astype(BF16)
            for part, v in enumerate((b0[0] * dc + b0[1] * ds, b0[1] * dc - b0[0] * ds)):
                v = jnp.broadcast_to((v * NORM).astype(BF16), (128, ROWS))
                mid[w, part] = nt(j, v)

    dx = [chirp_cols(level[w], i * CB, CB) for w in range(WL)]
    half = M // CB if CB < M else 1
    right = 4 + i * CB // M, pl.multiple_of(i % half * CB, CB)
    left = 3 - i * CB // M, pl.multiple_of((half - 1 - i % half) * CB, CB)
    for h in range(0, CB, SUB):
        cols = slice(h, h + SUB)
        for w in range(WL):
            for part in range(2):
                sp[w, part, :, cols] = nn(lhs[w, part], tab[w, 0, :, cols])
                sp[w, 2 + part, :, cols] = nn(lhs[w, 2 + part], tab[w, 1, :, cols])
        for r0 in range(0, ROWS, CHUNK):
            sl = slice(r0, r0 + CHUNK)
            tot = [0.0, 0.0, 0.0, 0.0]
            for w in range(WL):
                dc, ds = dx[w][0][:, cols], dx[w][1][:, cols]
                m = [jnp.concatenate([mid[w, part, sl, :]] * (SUB // 128), axis=1) for part in range(2)]
                cr, ci = sp[w, 0, sl, cols] + m[0], sp[w, 1, sl, cols] + m[1]
                sr, si = sp[w, 2, sl, cols], sp[w, 3, sl, cols]
                tot[0] += cr * dc + ci * ds
                tot[1] += ci * dc - cr * ds
                tot[2] += sr * dc + si * ds
                tot[3] += si * dc - sr * ds
            cr, ci, sr, si = tot
            g_r = (ci + sr) * fld[0, sl, cols] - (cr - si) * fld[1, sl, cols]
            g_l = (ci - sr) * fld[2, sl, cols] - (cr + si) * fld[3, sl, cols]
            out[right[0], sl, pl.ds(right[1] + h, SUB)] = g_r.astype(BF16)
            out[left[0], sl, pl.ds(left[1] + (CB - SUB - h), SUB)] = lane_rev(g_l).astype(BF16)


def run_forward(level, phase, aperture):
    smem = pl.BlockSpec(memory_space=pltpu.SMEM)
    right = pl.BlockSpec((ROWS, CB), lambda i: (0, HALF // CB + i))
    left = pl.BlockSpec((ROWS, CB), lambda i: (0, HALF // CB - 1 - i))
    return pl.pallas_call(
        forward_kernel,
        grid=(HALF // CB,),
        out_shape=(
            jax.ShapeDtypeStruct((WL, 2, K, HALF), BF16),
            jax.ShapeDtypeStruct((4, ROWS, HALF), F32),
            jax.ShapeDtypeStruct((16, WL * 2 * GRP, ROWS), BF16),
        ),
        in_specs=[smem, right, left, right, left],
        out_specs=(
            pl.BlockSpec((WL, 2, K, CB), lambda i: (0, 0, 0, i)),
            pl.BlockSpec((4, ROWS, CB), lambda i: (0, 0, i)),
            pl.BlockSpec((16, WL * 2 * GRP, ROWS), lambda i: (0, 0, 0)),
        ),
        scratch_shapes=[
            pltpu.VMEM((WL, 2, ROWS, CB), BF16),
            pltpu.VMEM((WL, 2, ROWS, CB), BF16),
            pltpu.VMEM((WL, 2, K + 16, ROWS), F32),
            pltpu.VMEM((WL, 2, K, ROWS), F32),
            pltpu.VMEM((K + 16, ROWS), F32),
        ],
        compiler_params=pltpu.CompilerParams(vmem_limit_bytes=60 * 2**20),
        name="forward",
    )(level, phase, phase, aperture, aperture)


def run_focal(x, tab, seen):
    return pl.pallas_call(
        focal_kernel,
        out_shape=jax.ShapeDtypeStruct((16, WL * 2 * GRP, ROWS), BF16),
        in_specs=[pl.BlockSpec(memory_space=pltpu.VMEM)] * 3,
        out_specs=pl.BlockSpec(memory_space=pltpu.VMEM),
        scratch_shapes=[pltpu.VMEM((WL, GRP, M), F32)],
        compiler_params=pltpu.CompilerParams(vmem_limit_bytes=60 * 2**20),
        name="focal",
    )(x, tab, seen)


def run_gradient(level, x, tab, fld):
    return pl.pallas_call(
        gradient_kernel,
        grid=(HALF // CB,),
        out_shape=jax.ShapeDtypeStruct((8, ROWS, M), BF16),
        in_specs=[
            pl.BlockSpec(memory_space=pltpu.SMEM),
            pl.BlockSpec((16, WL * 2 * GRP, ROWS), lambda i: (0, 0, 0)),
            pl.BlockSpec((WL, 2, K, CB), lambda i: (0, 0, 0, i)),
            pl.BlockSpec((4, ROWS, CB), lambda i: (0, 0, i)),
        ],
        out_specs=pl.BlockSpec((8, ROWS, M), lambda i: (0, 0, 0)),
        scratch_shapes=[
            pltpu.VMEM((WL, 4, ROWS, K), BF16),
            pltpu.VMEM((WL, 2, ROWS, 128), F32),
            pltpu.VMEM((WL, 4, ROWS, CB), F32),
            pltpu.VMEM((K + 8, ROWS), F32),
        ],
        compiler_params=pltpu.CompilerParams(vmem_limit_bytes=60 * 2**20),
        name="gradient",
    )(level, x, tab, fld)


def local(phase, aperture, defocus_index, intensity):
    level = defocus_index.astype(jnp.int32)
    tab, fld, sent = run_forward(level, phase, aperture)
    got = lax.all_to_all(sent, "row", 0, 0, tiled=True)
    sent = run_focal(got, tab, intensity)
    got = lax.all_to_all(sent, "row", 0, 0, tiled=True)
    parts = run_gradient(level, got, tab, fld)
    parts = lax.all_to_all(parts, "band", 0, 0, tiled=True)
    return jnp.sum(parts.astype(F32), axis=0)


def solution(mesh):
    return jax.shard_map(
        local,
        mesh=mesh,
        in_specs=(P("row", None), P("row", None), P("band"), P("band", "row", None)),
        out_specs=P("row", "band"),
        check_vma=False,
    )
```

time: 127 us -> 111 us (0.87)
  Pallas kernels: 41.8 us -> 30.9 us
  other arithmetic: 3.14 us -> 1.1 us
  local copies, waits for them, and re-layouts: 1.8 us -> 0 us
    pallas_call x2, Pallas kernels: 35.8 us -> 24.9 us  [the longest x1 14.1 us: run_forward(): pl.pallas_call(forward_kernel, grid=(HALF // CB,), out_shape=(jax.ShapeDt...]
    concatenate x2 -> x0, other arithmetic: 2.02 us -> none  [the longest x1 1.28 us: local(): jnp.concatenate([jnp.stack([row, band * WL]).astype(jnp.int32), defocus_i...]
    rev x2 -> x0, local copies, waits for them, and re-layouts: 1.71 us -> none  [the longest x1 1.54 us: fold(): turned = jnp.where(row < 8, jnp.flip(intensity, axis=1), intensity)]
where the time goes in v3:
time: 111 us; the launch traced here: 110 us
  blocking collectives  77.8 us (70%)
  Pallas kernels  30.9 us (28%)
    all_to_all x2, blocking collectives, local(): got = lax.all_to_all(sent, 'row', 0, 0, tiled=True)  48.8 us
    all_to_all x1, blocking collectives, local(): parts = lax.all_to_all(parts, 'band', 0, 0, tiled=True)  29 us
    pallas_call x1, Pallas kernels, run_forward(): pl.pallas_call(forward_kernel, grid=(HALF // CB,), out_shape=(jax.ShapeDt...  14.1 us
    pallas_call x1, Pallas kernels, run_gradient(): pl.pallas_call(gradient_kernel, grid=(HALF // CB,), out_shape=jax.ShapeDt...  10.8 us
    pallas_call x1, Pallas kernels, run_focal(): pl.pallas_call(focal_kernel, out_shape=jax.ShapeDtypeStruct((16, WL * 2 *...  5.95 us

profile of v3, /device:TPU:1, one launch (start us, length us, event | category | flops | bytes accessed | tf_op | source)
XLA Modules:
  0.0 109.8 jit_solution(8237911473762687106)
XLA Ops:
  0.0 14.1 %forward.1 = (bf16[2,2,256,2048]{3,2,1,0:T(8,128)(2,1)}, f32[4,256,2048]{2,1,0:T(8,128)}, bf16[16,128,256]{2,1,0:T(8,128)(2,1)}) custom-call(s32[2]{0:T(128)} %level.3, f32[256,4096]{1,0:T(8,128)} %ph_l.1, f32[256,4096]{1,0:T(8,128)} %ph_l.1, s32[256,4096]{1,0:T(8,128)} %ap_l.1, s32[256,4096]{1,0:T(8,128)} %ap_l.1), custom_call_target="tpu_custom_call" | custom-call | tf_op jit(solution)/shard_map/forward/pallas_call | solution.py:304
  14.1 26.5 %all_to_all.15.x = bf16[16,128,256]{2,1,0:T(8,128)(2,1)} all-to-all(bf16[16,128,256]{2,1,0:T(8,128)(2,1)} %get-tuple-element.8), channel_id=1, replica_groups=mesh['band'=8,'row'=16] {'row'}, dimensions={0} | all-to-all | bytes 2097152 | tf_op jit(solution)/shard_map/all_to_all | solution.py:368
  40.6 5.9 %focal.1 = bf16[16,128,256]{2,1,0:T(8,128)(2,1)} custom-call(bf16[16,128,256]{2,1,0:T(8,128)(2,1)} %all_to_all.15.x, bf16[2,2,256,2048]{3,2,1,0:T(8,128)(2,1)} %get-tuple-element.9.tab, f32[2,32,512]{2,1,0:T(8,128)} %seen.1), custom_call_target="tpu_custom_call" | custom-call | tf_op jit(solution)/shard_map/focal/pallas_call | solution.py:331
  46.6 22.3 %all_to_all.16.x = bf16[16,128,256]{2,1,0:T(8,128)(2,1)} all-to-all(bf16[16,128,256]{2,1,0:T(8,128)(2,1)} %focal.1), channel_id=1, replica_groups=mesh['band'=8,'row'=16] {'row'}, dimensions={0} | all-to-all | bytes 2097152 | tf_op jit(solution)/shard_map/all_to_all | solution.py:370
  68.9 10.8 %gradient.1 = bf16[8,256,512]{2,1,0:T(8,128)(2,1)} custom-call(s32[2]{0:T(128)} %level.3, bf16[16,128,256]{2,1,0:T(8,128)(2,1)} %all_to_all.16.x, bf16[2,2,256,2048]{3,2,1,0:T(8,128)(2,1)} %get-tuple-element.9.tab, f32[4,256,2048]{2,1,0:T(8,128)} %get-tuple-element.10.fld), custom_call_target="tpu_custom_call" | custom-call | tf_op jit(solution)/shard_map/gradient/pallas_call | solution.py:343
  79.7 29.0 %all_to_all.17 = bf16[8,256,512]{2,1,0:T(8,128)(2,1)S(1)} all-to-all(bf16[8,256,512]{2,1,0:T(8,128)(2,1)} %gradient.1), channel_id=1, replica_groups=mesh['band'=8,'row'=16] {'band'}, dimensions={0} | all-to-all | bytes 4194304 | tf_op jit(solution)/shard_map/all_to_all | solution.py:372
  108.7 1.1 convert_reduce_fusion

commit v4 on v3

--- a/solution.py
+++ b/solution.py
@@ -237,64 +237,68 @@
 
 
 def gradient_kernel(level, x, tab, fld, out, lhs, mid, sp, tmp):
-    i = pl.program_id(0)
     row = lax.axis_index("row")
-
-    @pl.when(i == 0)
-    def _():
-        flip = row < 8
-        j = flip_matrix(flip)
-        lane = lax.broadcasted_iota(jnp.int32, (1, ROWS), 1)
-        pos = row * ROWS + jnp.where(flip, ROWS - 1 - lane, lane)
-        for w in range(WL):
-            dc, ds = chirp_rows(level[w], pos)
-            p, m, b0 = [], [], []
-            for part in range(2):
-                at = (w * 2 + part) * GRP
-                for g in range(8):
-                    tmp[g * GRP : (g + 1) * GRP, :] = x[8 + g, at : at + GRP, :].astype(F32)
-                tmp[K : K + 8, :] = jnp.zeros((8, ROWS), F32)
-                b0.append(tmp[0:1, :])
-                p.append(tmp[pl.ds(1, K), :])
-                m.append(
-                    jnp.concatenate([x[7 - g, at : at + GRP, :] for g in range(8)], axis=0).astype(F32)
-                )
-            for n, (re, im) in enumerate(
-                ((p[0] + m[0], p[1] + m[1]), (p[0] - m[0], p[1] - m[1]))
-            ):
-                lhs[w, 2 * n] = nt(j, (re * dc + im * ds).astype(BF16)).astype(BF16)
-                lhs[w, 2 * n + 1] = nt(j, (im * dc - re * ds).astype(BF16)).astype(BF16)
-            for part, v in enumerate((b0[0] * dc + b0[1] * ds, b0[1] * dc - b0[0] * ds)):
-                v = jnp.broadcast_to((v * NORM).astype(BF16), (128, ROWS))
-                mid[w, part] = nt(j, v)
-
-    dx = [chirp_cols(level[w], i * CB, CB) for w in range(WL)]
-    half = M // CB if CB < M else 1
-    right = 4 + i * CB // M, pl.multiple_of(i % half * CB, CB)
-    left = 3 - i * CB // M, pl.multiple_of((half - 1 - i % half) * CB, CB)
-    for h in range(0, CB, SUB):
-        cols = slice(h, h + SUB)
-        for w in range(WL):
-            for part in range(2):
-                sp[w, part, :, cols] = nn(lhs[w, part], tab[w, 0, :, cols])
-                sp[w, 2 + part, :, cols] = nn(lhs[w, 2 + part], tab[w, 1, :, cols])
-        for r0 in range(0, ROWS, CHUNK):
-            sl = slice(r0, r0 + CHUNK)
-            tot = [0.0, 0.0, 0.0, 0.0]
+    flip = row < 8
+    j = flip_matrix(flip)
+    lane = lax.broadcasted_iota(jnp.int32, (1, ROWS), 1)
+    pos = row * ROWS + jnp.where(flip, ROWS - 1 - lane, lane)
+    for w in range(WL):
+        dc, ds = chirp_rows(level[w], pos)
+        p, m, b0 = [], [], []
+        for part in range(2):
+            at = (w * 2 + part) * GRP
+            for g in range(8):
+                tmp[g * GRP : (g + 1) * GRP, :] = x[8 + g, at : at + GRP, :].astype(F32)
+            tmp[K : K + 8, :] = jnp.zeros((8, ROWS), F32)
+            b0.append(tmp[0:1, :])
+            p.append(tmp[pl.ds(1, K), :])
+            m.append(
+                jnp.concatenate([x[7 - g, at : at + GRP, :] for g in range(8)], axis=0).astype(F32)
+            )
+        for n, (re, im) in enumerate(
+            ((p[0] + m[0], p[1] + m[1]), (p[0] - m[0], p[1] - m[1]))
+        ):
+            lhs[w, 2 * n] = nt(j, (re * dc + im * ds).astype(BF16)).astype(BF16)
+            lhs[w, 2 * n + 1] = nt(j, (im * dc - re * ds).astype(BF16)).astype(BF16)
+        for part, v in enumerate((b0[0] * dc + b0[1] * ds, b0[1] * dc - b0[0] * ds)):
+            v = jnp.broadcast_to((v * NORM).astype(BF16), (128, ROWS))
+            mid[w, part] = nt(j, v)
+
+    def block(i, _):
+        base = pl.multiple_of(i * CB, CB)
+        dx = [chirp_cols(level[w], base, CB) for w in range(WL)]
+        per = M // CB
+        right = 4 + i // per, pl.multiple_of(i % per * CB, CB)
+        left = 3 - i // per, pl.multiple_of((per - 1 - i % per) * CB, CB)
+        for h in range(0, CB, SUB):
+            cols = pl.ds(pl.multiple_of(base + h, SUB), SUB)
             for w in range(WL):
-                dc, ds = dx[w][0][:, cols], dx[w][1][:, cols]
-                m = [jnp.concatenate([mid[w, part, sl, :]] * (SUB // 128), axis=1) for part in range(2)]
-                cr, ci = sp[w, 0, sl, cols] + m[0], sp[w, 1, sl, cols] + m[1]
-                sr, si = sp[w, 2, sl, cols], sp[w, 3, sl, cols]
-                tot[0] += cr * dc + ci * ds
-                tot[1] += ci * dc - cr * ds
-                tot[2] += sr * dc + si * ds
-                tot[3] += si * dc - sr * ds
-            cr, ci, sr, si = tot
-            g_r = (ci + sr) * fld[0, sl, cols] - (cr - si) * fld[1, sl, cols]
-            g_l = (ci - sr) * fld[2, sl, cols] - (cr + si) * fld[3, sl, cols]
-            out[right[0], sl, pl.ds(right[1] + h, SUB)] = g_r.astype(BF16)
-            out[left[0], sl, pl.ds(left[1] + (CB - SUB - h), SUB)] = lane_rev(g_l).astype(BF16)
+                for part in range(2):
+                    sp[w, part, :, h : h + SUB] = nn(lhs[w, part], tab[w, 0, :, cols])
+                    sp[w, 2 + part, :, h : h + SUB] = nn(lhs[w, 2 + part], tab[w, 1, :, cols])
+            for r0 in range(0, ROWS, CHUNK):
+                sl = slice(r0, r0 + CHUNK)
+                tot = [0.0, 0.0, 0.0, 0.0]
+                for w in range(WL):
+                    dc, ds = dx[w][0][:, h : h + SUB], dx[w][1][:, h : h + SUB]
+                    m = [
+                        jnp.concatenate([mid[w, part, sl, :]] * (SUB // 128), axis=1)
+                        for part in range(2)
+                    ]
+                    cr, ci = sp[w, 0, sl, h : h + SUB] + m[0], sp[w, 1, sl, h : h + SUB] + m[1]
+                    sr, si = sp[w, 2, sl, h : h + SUB], sp[w, 3, sl, h : h + SUB]
+                    tot[0] += cr * dc + ci * ds
+                    tot[1] += ci * dc - cr * ds
+                    tot[2] += sr * dc + si * ds
+                    tot[3] += si * dc - sr * ds
+                cr, ci, sr, si = tot
+                g_r = (ci + sr) * fld[0, sl, cols] - (cr - si) * fld[1, sl, cols]
+                g_l = (ci - sr) * fld[2, sl, cols] - (cr + si) * fld[3, sl, cols]
+                out[right[0], sl, pl.ds(right[1] + h, SUB)] = g_r.astype(BF16)
+                out[left[0], sl, pl.ds(left[1] + (CB - SUB - h), SUB)] = lane_rev(g_l).astype(BF16)
+        return 0
+
+    lax.fori_loop(0, HALF // CB, block, 0)
 
 
 def run_forward(level, phase, aperture):
@@ -334,7 +338,8 @@
         in_specs=[pl.BlockSpec(memory_space=pltpu.VMEM)] * 3,
         out_specs=pl.BlockSpec(memory_space=pltpu.VMEM),
         scratch_shapes=[pltpu.VMEM((WL, GRP, M), F32)],
-        compiler_params=pltpu.CompilerParams(vmem_limit_bytes=60 * 2**20),
+        compiler_params=pltpu.CompilerParams(vmem_limit_bytes=20 * 2**20),
+        cost_estimate=pl.CostEstimate(flops=2**34, bytes_accessed=2**26, transcendentals=0),
         name="focal",
     )(x, tab, seen)
 
@@ -342,22 +347,17 @@
 def run_gradient(level, x, tab, fld):
     return pl.pallas_call(
         gradient_kernel,
-        grid=(HALF // CB,),
         out_shape=jax.ShapeDtypeStruct((8, ROWS, M), BF16),
-        in_specs=[
-            pl.BlockSpec(memory_space=pltpu.SMEM),
-            pl.BlockSpec((16, WL * 2 * GRP, ROWS), lambda i: (0, 0, 0)),
-            pl.BlockSpec((WL, 2, K, CB), lambda i: (0, 0, 0, i)),
-            pl.BlockSpec((4, ROWS, CB), lambda i: (0, 0, i)),
-        ],
-        out_specs=pl.BlockSpec((8, ROWS, M), lambda i: (0, 0, 0)),
+        in_specs=[pl.BlockSpec(memory_space=pltpu.SMEM)] + [pl.BlockSpec(memory_space=pltpu.VMEM)] * 3,
+        out_specs=pl.BlockSpec(memory_space=pltpu.VMEM),
         scratch_shapes=[
             pltpu.VMEM((WL, 4, ROWS, K), BF16),
             pltpu.VMEM((WL, 2, ROWS, 128), F32),
             pltpu.VMEM((WL, 4, ROWS, CB), F32),
             pltpu.VMEM((K + 8, ROWS), F32),
         ],
-        compiler_params=pltpu.CompilerParams(vmem_limit_bytes=60 * 2**20),
+        compiler_params=pltpu.CompilerParams(vmem_limit_bytes=28 * 2**20),
+        cost_estimate=pl.CostEstimate(flops=2**34, bytes_accessed=2**26, transcendentals=0),
         name="gradient",
     )(level, x, tab, fld)
 

time: 111 us -> 106 us (0.955)
  Pallas kernels: 30.9 us -> 24.4 us
  local copies, waits for them, and re-layouts: 0 us -> 2.21 us
  blocking collectives: 77.8 us -> 76.2 us
    pallas_call x1, Pallas kernels: 5.95 us -> 2.42 us  [run_focal(): pl.pallas_call(focal_kernel, out_shape=jax.ShapeDtypeStruct((16, WL * 2 *...]
    pallas_call x1, Pallas kernels: 10.8 us -> 7.81 us  [run_gradient(): pl.pallas_call(gradient_kernel, out_shape=jax.ShapeDtypeStruct((8, ROWS,...]
    unnamed x0 -> x12, local copies, waits for them, and re-layouts: none -> 2.21 us
    all_to_all x2, blocking collectives: 48.8 us -> 47.4 us  [local(): got = lax.all_to_all(sent, 'row', 0, 0, tiled=True)]
where the time goes in v4:
time: 106 us; the launch traced here: 104 us
  blocking collectives  76.2 us (72%)
  Pallas kernels  24.4 us (23%)
  local copies, waits for them, and re-layouts  2.21 us (2%)
  other arithmetic  1.1 us (1%)
    all_to_all x2, blocking collectives, local(): got = lax.all_to_all(sent, 'row', 0, 0, tiled=True)  47.4 us
    all_to_all x1, blocking collectives, local(): parts = lax.all_to_all(parts, 'band', 0, 0, tiled=True)  28.8 us
    pallas_call x1, Pallas kernels, run_forward(): pl.pallas_call(forward_kernel, grid=(HALF // CB,), out_shape=(jax.ShapeDt...  14.2 us
    pallas_call x1, Pallas kernels, run_gradient(): pl.pallas_call(gradient_kernel, out_shape=jax.ShapeDtypeStruct((8, ROWS,...  7.81 us
    pallas_call x1, Pallas kernels, run_focal(): pl.pallas_call(focal_kernel, out_shape=jax.ShapeDtypeStruct((16, WL * 2 *...  2.42 us
    unnamed x12, local copies, waits for them, and re-layouts  2.21 us

profile of v4, /device:TPU:1, one launch (start us, length us, event | category | flops | bytes accessed | tf_op | source)
XLA Modules:
  0.0 103.9 jit_solution(6640167754387375668)
XLA Ops:
  0.0 0.0 copy-start.3
  0.0 14.2 %forward.1 = (bf16[2,2,256,2048]{3,2,1,0:T(8,128)(2,1)}, f32[4,256,2048]{2,1,0:T(8,128)}, bf16[16,128,256]{2,1,0:T(8,128)(2,1)}) custom-call(s32[2]{0:T(128)} %level.3, f32[256,4096]{1,0:T(8,128)} %ph_l.1, f32[256,4096]{1,0:T(8,128)} %ph_l.1, s32[256,4096]{1,0:T(8,128)} %ap_l.1, s32[256,4096]{1,0:T(8,128)} %ap_l.1), custom_call_target="tpu_custom_call" | custom-call | tf_op jit(solution)/shard_map/forward/pallas_call | solution.py:308
  14.2 0.0 slice-start
  14.2 26.6 %all_to_all.15.x = bf16[16,128,256]{2,1,0:T(8,128)(2,1)S(1)} all-to-all(bf16[16,128,256]{2,1,0:T(8,128)(2,1)} %get-tuple-element.8), channel_id=1, replica_groups=mesh['band'=8,'row'=16] {'row'}, dimensions={0} | all-to-all | bytes 2097152 | tf_op jit(solution)/shard_map/all_to_all | solution.py:368
  40.8 0.0 copy-done.3
  40.8 0.0 copy-start.1
  40.8 2.2 %copy-done.1 = bf16[2,2,256,2048]{3,2,1,0:T(8,128)(2,1)S(1)} copy-done((bf16[2,2,256,2048]{3,2,1,0:T(8,128)(2,1)S(1)}, bf16[2,2,256,2048]{3,2,1,0:T(8,128)(2,1)}, u32[]{:S(2)}) %copy-start.1) | copy-done | bytes 4194328
  43.0 0.0 copy-start
  43.0 0.0 slice-start.1
  43.0 0.0 copy-start.2
  43.0 2.4 %focal.1 = bf16[16,128,256]{2,1,0:T(8,128)(2,1)S(1)} custom-call(bf16[16,128,256]{2,1,0:T(8,128)(2,1)S(1)} %all_to_all.15.x, bf16[2,2,256,2048]{3,2,1,0:T(8,128)(2,1)S(1)} %copy-done.1, f32[2,32,512]{2,1,0:T(8,128)S(1)} %copy-done.3), custom_call_target="tpu_custom_call" | custom-call | flops 17179869184 | bytes 67108864 | tf_op jit(solution)/shard_map/focal/pallas_call | solution.py:335
  45.5 20.7 %all_to_all.16.x = bf16[16,128,256]{2,1,0:T(8,128)(2,1)S(1)} all-to-all(bf16[16,128,256]{2,1,0:T(8,128)(2,1)S(1)} %focal.1), channel_id=1, replica_groups=mesh['band'=8,'row'=16] {'row'}, dimensions={0} | all-to-all | bytes 2097152 | tf_op jit(solution)/shard_map/all_to_all | solution.py:370
  66.2 0.0 slice-done
  66.2 0.0 copy-done
  66.2 0.0 slice-done.1
  66.2 0.0 copy-done.2
  66.2 7.8 %gradient.1 = bf16[8,256,512]{2,1,0:T(8,128)(2,1)S(1)} custom-call(s32[2]{0:T(128)S(1)} %copy-done, bf16[16,128,256]{2,1,0:T(8,128)(2,1)S(1)} %all_to_all.16.x, bf16[2,2,256,2048]{3,2,1,0:T(8,128)(2,1)S(1)} %copy-done.2, f32[4,256,2048]{2,1,0:T(8,128)S(1)} %bitcast.1), custom_call_target="tpu_custom_call" | custom-call | flops 17179869184 | bytes 67108864 | tf_op jit(solution)/shard_map/gradient/pallas_call | solution.py:348
  74.0 28.8 %all_to_all.17 = bf16[8,256,512]{2,1,0:T(8,128)(2,1)S(1)} all-to-all(bf16[8,256,512]{2,1,0:T(8,128)(2,1)S(1)} %gradient.1), channel_id=1, replica_groups=mesh['band'=8,'row'=16] {'band'}, dimensions={0} | all-to-all | bytes 4194304 | tf_op jit(solution)/shard_map/all_to_all | solution.py:372
  102.8 1.1 %convert_reduce_fusion = f32[256,512]{1,0:T(8,128)} fusion(bf16[8,256,512]{2,1,0:T(8,128)(2,1)S(1)} %all_to_all.17), kind=kLoop, calls=%fused_computation | loop fusion | flops 1966080 | bytes 2621440 | tf_op jit(solution)/shard_map/reduce_sum | solution.py:373
  (1 shorter events, 0.0 us)
Async XLA Ops:
  0.0 40.8 %copy-start.3 = (f32[2,32,512]{2,1,0:T(8,128)S(1)}, f32[2,32,512]{2,1,0:T(8,128)}, u32[]{:S(2)}) copy-start(f32[2,32,512]{2,1,0:T(8,128)} %seen.1) | copy-start | bytes 393220
  14.2 52.0 %slice-start = ((s8[8388608]{0:T(1024)(128)(4,1)}), s8[4194304]{0:T(1024)(128)(4,1)S(1)}, s32[]{:S(2)}) async-start(s8[8388608]{0:T(1024)(128)(4,1)} %bitcast), calls=%async_computation.3 | async-start | bytes 8388608
  40.8 2.2 %copy-start.1 = (bf16[2,2,256,2048]{3,2,1,0:T(8,128)(2,1)S(1)}, bf16[2,2,256,2048]{3,2,1,0:T(8,128)(2,1)}, u32[]{:S(2)}) copy-start(bf16[2,2,256,2048]{3,2,1,0:T(8,128)(2,1)} %get-tuple-element.9.tab) | copy-start | bytes 12582916
  43.0 23.2 %copy-start = (s32[2]{0:T(128)S(1)}, s32[2]{0:T(128)}, u32[]{:S(2)}) copy-start(s32[2]{0:T(128)} %level.3) | copy-start | bytes 28
  43.0 23.2 %slice-start.1 = ((s8[8388608]{0:T(1024)(128)(4,1)}), s8[4194304]{0:T(1024)(128)(4,1)S(1)}, s32[]{:S(2)}) async-start(s8[8388608]{0:T(1024)(128)(4,1)} %bitcast), calls=%async_computation.4 | async-start | bytes 8388608
  43.0 23.2 %copy-start.2 = (bf16[2,2,256,2048]{3,2,1,0:T(8,128)(2,1)S(1)}, bf16[2,2,256,2048]{3,2,1,0:T(8,128)(2,1)}, u32[]{:S(2)}) copy-start(bf16[2,2,256,2048]{3,2,1,0:T(8,128)(2,1)} %get-tuple-element.9.tab) | copy-start | bytes 12582916

commit v5 on v4

--- a/solution.py
+++ b/solution.py
@@ -5,6 +5,7 @@
 from jax import lax
 from jax.experimental import pallas as pl
 from jax.experimental.pallas import tpu as pltpu
+from jax.sharding import Mesh
 from jax.sharding import PartitionSpec as P
 
 F32 = jnp.float32
@@ -21,6 +22,8 @@
 STEPS = HALF // BLK
 WL = 2
 GRP = 32
+PAIR = 2
+PART = ROWS // PAIR
 NORM = 1.0 / math.sqrt(N)
 
 SIN_C = (9.99999246e-01, -1.66656827e-01, 8.31325871e-03, -1.85243573e-04)
@@ -75,7 +78,9 @@
 
 
 def span(w):
-    return (1024 * (16 + lax.axis_index("band") * WL + w)).astype(F32)
+    lo = lax.axis_index("band_lo")
+    wave = lax.axis_index("band_hi") * (PAIR * WL) + (lo * WL + w) % (PAIR * WL)
+    return (1024 * (16 + wave)).astype(F32)
 
 
 def angle(n, m):
@@ -94,18 +99,18 @@
     return turn(x * x * (level.astype(F32) * (0.5 / (N * N))))
 
 
-def flip_matrix(flip):
-    r = lax.broadcasted_iota(jnp.int32, (ROWS, ROWS), 0)
-    c = lax.broadcasted_iota(jnp.int32, (ROWS, ROWS), 1)
-    return jnp.where(jnp.where(flip, ROWS - 1 - c, c) == r, 1.0, 0.0).astype(BF16)
-
-
-def write_tables(tab, first):
+def flip_matrix(flip, size):
+    r = lax.broadcasted_iota(jnp.int32, (size, size), 0)
+    c = lax.broadcasted_iota(jnp.int32, (size, size), 1)
+    return jnp.where(jnp.where(flip, size - 1 - c, c) == r, 1.0, 0.0).astype(BF16)
+
+
+def write_tables(tab, first, wave0):
     k = lax.broadcasted_iota(jnp.int32, (8, 128), 0) + 1
     lane = lax.broadcasted_iota(jnp.int32, (8, 128), 1)
     at, state = [], []
     for w in range(WL):
-        m = span(w)
+        m = span(wave0 + w)
         for t in range(0, CB, 128):
             x = 2 * (first + t + lane) + 1
             c, s = angle((x * k).astype(F32), m)
@@ -122,47 +127,56 @@
             state[n] = (c1 * rc - s1 * rs, c1 * rs + s1 * rc, rc, rs)
 
 
-def forward_kernel(level, ph_r, ph_l, ap_r, ap_l, tab, fld, out, e_s, o_s, xacc, yacc, tmp):
+def forward_kernel(level, ph_r, ph_l, ap_r, ap_l, tab, tab2, fld, out, *scratch):
+    n_sub = CB // SUB
+    e_all, o_all = scratch[:n_sub], scratch[n_sub : 2 * n_sub]
+    xacc, yacc, tmp = scratch[2 * n_sub :]
     i = pl.program_id(0)
     row = lax.axis_index("row")
+    mine = lax.axis_index("band_lo") * PART
 
     @pl.when(i == 0)
     def _():
         xacc[...] = jnp.zeros_like(xacc)
         yacc[...] = jnp.zeros_like(yacc)
 
-    write_tables(tab, i * CB)
+    write_tables(tab, i * CB, 0)
+    write_tables(tab2, i * CB, WL)
     dx = [chirp_cols(level[w], i * CB, CB) for w in range(WL)]
     ones = jnp.full((16, SUB), NORM, BF16)
-    for h in range(0, CB, SUB):
+    for n in range(n_sub):
+        h = n * SUB
+        e_s, o_s = e_all[n], o_all[n]
         cols = slice(h, h + SUB)
         mirror = slice(CB - SUB - h, CB - h)
         for r0 in range(0, ROWS, CHUNK):
-            sl = slice(r0, r0 + CHUNK)
+            sl = pl.ds(pl.multiple_of((mine + r0) % ROWS, CHUNK), CHUNK)
             fr_c, fr_s = field(ph_r[sl, cols], ap_r[sl, cols].astype(F32))
             fl_c, fl_s = field(lane_rev(ph_l[sl, mirror]), lane_rev(ap_l[sl, mirror]).astype(F32))
-            fld[0, sl, cols] = fr_c
-            fld[1, sl, cols] = fr_s
-            fld[2, sl, cols] = fl_c
-            fld[3, sl, cols] = fl_s
+            if r0 < PART:
+                keep = slice(r0, r0 + CHUNK)
+                fld[0, keep, cols] = fr_c
+                fld[1, keep, cols] = fr_s
+                fld[2, keep, cols] = fl_c
+                fld[3, keep, cols] = fl_s
             ec, es = fr_c + fl_c, fr_s + fl_s
             oc, os = fr_c - fl_c, fr_s - fl_s
             for w in range(WL):
                 dc, ds = dx[w][0][:, cols], dx[w][1][:, cols]
-                e_s[w, 0, sl, cols] = (ec * dc - es * ds).astype(BF16)
-                e_s[w, 1, sl, cols] = (ec * ds + es * dc).astype(BF16)
-                o_s[w, 0, sl, cols] = (oc * dc - os * ds).astype(BF16)
-                o_s[w, 1, sl, cols] = (oc * ds + os * dc).astype(BF16)
+                e_s[w, 0, sl, :] = (ec * dc - es * ds).astype(BF16)
+                e_s[w, 1, sl, :] = (ec * ds + es * dc).astype(BF16)
+                o_s[w, 0, sl, :] = (oc * dc - os * ds).astype(BF16)
+                o_s[w, 1, sl, :] = (oc * ds + os * dc).astype(BF16)
         for w in range(WL):
             c = jnp.concatenate([tab[w, 0, :, cols], ones], axis=0)
             s = tab[w, 1, :, cols]
             for part in range(2):
-                xacc[w, part] += nt(c, e_s[w, part, :, cols])
-                yacc[w, part] += nt(s, o_s[w, part, :, cols])
+                xacc[w, part] += nt(c, e_s[w, part])
+                yacc[w, part] += nt(s, o_s[w, part])
 
     @pl.when(i == HALF // CB - 1)
     def _():
-        j = flip_matrix(row < 8)
+        j = flip_matrix(row < 8, ROWS)
         pos = row * ROWS + lax.broadcasted_iota(jnp.int32, (1, ROWS), 1)
         for w in range(WL):
             dc, ds = chirp_rows(level[w], pos)
@@ -230,63 +244,69 @@
             bc = nn(s, tab[w, 0, :, cols]) + centre
             bs = nn(d, tab[w, 1, :, cols])
             bcr, bci, bsr, bsi = bc[:GRP], bc[GRP:], bs[:GRP], bs[GRP:]
-            out[8 + i, at : at + GRP, :] = (bcr - bsi).astype(BF16)
-            out[8 + i, at + GRP : at + 2 * GRP, :] = (bci + bsr).astype(BF16)
-            out[7 - i, at : at + GRP, :] = (bcr + bsi).astype(BF16)
-            out[7 - i, at + GRP : at + 2 * GRP, :] = (bci - bsr).astype(BF16)
-
-
-def gradient_kernel(level, x, tab, fld, out, lhs, mid, sp, tmp):
+            for block, re, im in ((8 + i, bcr - bsi, bci + bsr), (7 - i, bcr + bsi, bci - bsr)):
+                re, im = re.astype(BF16), im.astype(BF16)
+                for q in range(PAIR):
+                    p = q if block >= 8 else PAIR - 1 - q
+                    lanes = slice(p * PART, (p + 1) * PART)
+                    out[q * 16 + block, at : at + GRP, :] = re[:, lanes]
+                    out[q * 16 + block, at + GRP : at + 2 * GRP, :] = im[:, lanes]
+
+
+def gradient_kernel(level, x, tab, tab2, fld, out, lhs, mid, sp, tmp):
     row = lax.axis_index("row")
+    lo = lax.axis_index("band_lo")
     flip = row < 8
-    j = flip_matrix(flip)
-    lane = lax.broadcasted_iota(jnp.int32, (1, ROWS), 1)
-    pos = row * ROWS + jnp.where(flip, ROWS - 1 - lane, lane)
-    for w in range(WL):
+    j = flip_matrix(flip, PART)
+    lane = lax.broadcasted_iota(jnp.int32, (1, PART), 1)
+    pos = row * ROWS + lo * PART + jnp.where(flip, PART - 1 - lane, lane)
+    for w in range(PAIR * WL):
+        src = (lo + w // WL) % PAIR * 16
         dc, ds = chirp_rows(level[w], pos)
         p, m, b0 = [], [], []
         for part in range(2):
-            at = (w * 2 + part) * GRP
+            at = (w % WL * 2 + part) * GRP
             for g in range(8):
-                tmp[g * GRP : (g + 1) * GRP, :] = x[8 + g, at : at + GRP, :].astype(F32)
-            tmp[K : K + 8, :] = jnp.zeros((8, ROWS), F32)
+                tmp[g * GRP : (g + 1) * GRP, :] = x[src + 8 + g, at : at + GRP, :].astype(F32)
+            tmp[K : K + 8, :] = jnp.zeros((8, PART), F32)
             b0.append(tmp[0:1, :])
             p.append(tmp[pl.ds(1, K), :])
             m.append(
-                jnp.concatenate([x[7 - g, at : at + GRP, :] for g in range(8)], axis=0).astype(F32)
+                jnp.concatenate([x[src + 7 - g, at : at + GRP, :] for g in range(8)], axis=0).astype(F32)
             )
         for n, (re, im) in enumerate(
             ((p[0] + m[0], p[1] + m[1]), (p[0] - m[0], p[1] - m[1]))
         ):
-            lhs[w, 2 * n] = nt(j, (re * dc + im * ds).astype(BF16)).astype(BF16)
-            lhs[w, 2 * n + 1] = nt(j, (im * dc - re * ds).astype(BF16)).astype(BF16)
+            lhs[w, n, :PART] = nt(j, (re * dc + im * ds).astype(BF16)).astype(BF16)
+            lhs[w, n, PART:] = nt(j, (im * dc - re * ds).astype(BF16)).astype(BF16)
         for part, v in enumerate((b0[0] * dc + b0[1] * ds, b0[1] * dc - b0[0] * ds)):
-            v = jnp.broadcast_to((v * NORM).astype(BF16), (128, ROWS))
+            v = jnp.broadcast_to((v * NORM).astype(BF16), (128, PART))
             mid[w, part] = nt(j, v)
 
     def block(i, _):
         base = pl.multiple_of(i * CB, CB)
-        dx = [chirp_cols(level[w], base, CB) for w in range(WL)]
+        dx = [chirp_cols(level[w], base, CB) for w in range(PAIR * WL)]
         per = M // CB
         right = 4 + i // per, pl.multiple_of(i % per * CB, CB)
         left = 3 - i // per, pl.multiple_of((per - 1 - i % per) * CB, CB)
         for h in range(0, CB, SUB):
             cols = pl.ds(pl.multiple_of(base + h, SUB), SUB)
-            for w in range(WL):
-                for part in range(2):
-                    sp[w, part, :, h : h + SUB] = nn(lhs[w, part], tab[w, 0, :, cols])
-                    sp[w, 2 + part, :, h : h + SUB] = nn(lhs[w, 2 + part], tab[w, 1, :, cols])
-            for r0 in range(0, ROWS, CHUNK):
+            for w in range(PAIR * WL):
+                table = tab if w < WL else tab2
+                for n in range(2):
+                    sp[w, n, :, h : h + SUB] = nn(lhs[w, n], table[w % WL, n, :, cols])
+            for r0 in range(0, PART, CHUNK):
                 sl = slice(r0, r0 + CHUNK)
+                im = slice(PART + r0, PART + r0 + CHUNK)
                 tot = [0.0, 0.0, 0.0, 0.0]
-                for w in range(WL):
+                for w in range(PAIR * WL):
                     dc, ds = dx[w][0][:, h : h + SUB], dx[w][1][:, h : h + SUB]
                     m = [
                         jnp.concatenate([mid[w, part, sl, :]] * (SUB // 128), axis=1)
                         for part in range(2)
                     ]
-                    cr, ci = sp[w, 0, sl, h : h + SUB] + m[0], sp[w, 1, sl, h : h + SUB] + m[1]
-                    sr, si = sp[w, 2, sl, h : h + SUB], sp[w, 3, sl, h : h + SUB]
+                    cr, ci = sp[w, 0, sl, h : h + SUB] + m[0], sp[w, 0, im, h : h + SUB] + m[1]
+                    sr, si = sp[w, 1, sl, h : h + SUB], sp[w, 1, im, h : h + SUB]
                     tot[0] += cr * dc + ci * ds
                     tot[1] += ci * dc - cr * ds
                     tot[2] += sr * dc + si * ds
@@ -310,18 +330,19 @@
         grid=(HALF // CB,),
         out_shape=(
             jax.ShapeDtypeStruct((WL, 2, K, HALF), BF16),
-            jax.ShapeDtypeStruct((4, ROWS, HALF), F32),
+            jax.ShapeDtypeStruct((WL, 2, K, HALF), BF16),
+            jax.ShapeDtypeStruct((4, PART, HALF), F32),
             jax.ShapeDtypeStruct((16, WL * 2 * GRP, ROWS), BF16),
         ),
         in_specs=[smem, right, left, right, left],
         out_specs=(
             pl.BlockSpec((WL, 2, K, CB), lambda i: (0, 0, 0, i)),
-            pl.BlockSpec((4, ROWS, CB), lambda i: (0, 0, i)),
+            pl.BlockSpec((WL, 2, K, CB), lambda i: (0, 0, 0, i)),
+            pl.BlockSpec((4, PART, CB), lambda i: (0, 0, i)),
             pl.BlockSpec((16, WL * 2 * GRP, ROWS), lambda i: (0, 0, 0)),
         ),
-        scratch_shapes=[
-            pltpu.VMEM((WL, 2, ROWS, CB), BF16),
-            pltpu.VMEM((WL, 2, ROWS, CB), BF16),
+        scratch_shapes=[pltpu.VMEM((WL, 2, ROWS, SUB), BF16)] * (2 * CB // SUB)
+        + [
             pltpu.VMEM((WL, 2, K + 16, ROWS), F32),
             pltpu.VMEM((WL, 2, K, ROWS), F32),
             pltpu.VMEM((K + 16, ROWS), F32),
@@ -334,7 +355,7 @@
 def run_focal(x, tab, seen):
     return pl.pallas_call(
         focal_kernel,
-        out_shape=jax.ShapeDtypeStruct((16, WL * 2 * GRP, ROWS), BF16),
+        out_shape=jax.ShapeDtypeStruct((PAIR * 16, WL * 2 * GRP, PART), BF16),
         in_specs=[pl.BlockSpec(memory_space=pltpu.VMEM)] * 3,
         out_specs=pl.BlockSpec(memory_space=pltpu.VMEM),
         scratch_shapes=[pltpu.VMEM((WL, GRP, M), F32)],
@@ -344,40 +365,45 @@
     )(x, tab, seen)
 
 
-def run_gradient(level, x, tab, fld):
+def run_gradient(level, x, tab, tab2, fld):
     return pl.pallas_call(
         gradient_kernel,
-        out_shape=jax.ShapeDtypeStruct((8, ROWS, M), BF16),
-        in_specs=[pl.BlockSpec(memory_space=pltpu.SMEM)] + [pl.BlockSpec(memory_space=pltpu.VMEM)] * 3,
+        out_shape=jax.ShapeDtypeStruct((8, PART, M), BF16),
+        in_specs=[pl.BlockSpec(memory_space=pltpu.SMEM)] + [pl.BlockSpec(memory_space=pltpu.VMEM)] * 4,
         out_specs=pl.BlockSpec(memory_space=pltpu.VMEM),
         scratch_shapes=[
-            pltpu.VMEM((WL, 4, ROWS, K), BF16),
-            pltpu.VMEM((WL, 2, ROWS, 128), F32),
-            pltpu.VMEM((WL, 4, ROWS, CB), F32),
-            pltpu.VMEM((K + 8, ROWS), F32),
+            pltpu.VMEM((PAIR * WL, 2, 2 * PART, K), BF16),
+            pltpu.VMEM((PAIR * WL, 2, PART, 128), F32),
+            pltpu.VMEM((PAIR * WL, 2, 2 * PART, CB), F32),
+            pltpu.VMEM((K + 8, PART), F32),
         ],
         compiler_params=pltpu.CompilerParams(vmem_limit_bytes=28 * 2**20),
         cost_estimate=pl.CostEstimate(flops=2**34, bytes_accessed=2**26, transcendentals=0),
         name="gradient",
-    )(level, x, tab, fld)
+    )(level, x, tab, tab2, fld)
 
 
 def local(phase, aperture, defocus_index, intensity):
     level = defocus_index.astype(jnp.int32)
-    tab, fld, sent = run_forward(level, phase, aperture)
+    levels = jnp.concatenate([level, lax.ppermute(level, "band_lo", [(0, 1), (1, 0)])])
+    tab, tab2, fld, sent = run_forward(level, phase, aperture)
+    sent, levels = lax.optimization_barrier((sent, levels))
     got = lax.all_to_all(sent, "row", 0, 0, tiled=True)
     sent = run_focal(got, tab, intensity)
-    got = lax.all_to_all(sent, "row", 0, 0, tiled=True)
-    parts = run_gradient(level, got, tab, fld)
-    parts = lax.all_to_all(parts, "band", 0, 0, tiled=True)
-    return jnp.sum(parts.astype(F32), axis=0)
+    got = lax.all_to_all(sent, ("band_lo", "row"), 0, 0, tiled=True)
+    parts = run_gradient(levels, got, tab, tab2, fld)
+    parts = lax.all_to_all(parts, ("band_hi", "band_lo"), 0, 0, tiled=True)
+    return jnp.sum(parts.reshape(8 // PAIR, ROWS, M).astype(F32), axis=0)
 
 
 def solution(mesh):
+    band, row = mesh.devices.shape
+    split = Mesh(mesh.devices.reshape(band // PAIR, PAIR, row), ("band_hi", "band_lo", "row"))
+    both = ("band_hi", "band_lo")
     return jax.shard_map(
         local,
-        mesh=mesh,
-        in_specs=(P("row", None), P("row", None), P("band"), P("band", "row", None)),
-        out_specs=P("row", "band"),
+        mesh=split,
+        in_specs=(P("row", None), P("row", None), P(both), P(both, "row", None)),
+        out_specs=P("row", both),
         check_vma=False,
     )

time: 106 us -> 96.3 us (0.908); the launches traced: 104 us -> 96.1 us
  blocking collectives: 76.2 us -> 65.7 us
  starting transfers between devices: 0 us -> 2.13 us
    all_to_all x2 -> x1, blocking collectives: 47.4 us -> 25.5 us  [local(): got = lax.all_to_all(sent, 'row', 0, 0, tiled=True)]
    all_to_all x1 -> x2, blocking collectives: 28.8 us -> 40.1 us  [the longest x1 21.3 us: local(): got = lax.all_to_all(sent, ('band_lo', 'row'), 0, 0, tiled=True)]
    ppermute x0 -> x1, starting transfers between devices: none -> 2.13 us  [local(): lax.ppermute(level, 'band_lo', [(0, 1), (1, 0)])]
    pallas_call x1, Pallas kernels: 14.2 us -> 15.3 us  [run_forward(): pl.pallas_call(forward_kernel, grid=(HALF // CB,), out_shape=(jax.ShapeDt...]
  transfers between devices with their start and end apart: 0 -> 1, of which waited for: 0 -> 0; matrix products, arithmetic and copies ran while one was open for 0% -> 0% of each run, Pallas kernels for 0% -> 16%
where the time goes in v5:
time: 96.3 us; the launch traced here: 96.1 us
  blocking collectives  65.7 us (68%)
  Pallas kernels  25 us (26%)
  local copies, waits for them, and re-layouts  2.21 us (2%)
  starting transfers between devices  2.13 us (2%)
  other arithmetic  1.01 us (1%)
    all_to_all x1, blocking collectives, local(): got = lax.all_to_all(sent, 'row', 0, 0, tiled=True)  25.5 us
    all_to_all x1, blocking collectives, local(): got = lax.all_to_all(sent, ('band_lo', 'row'), 0, 0, tiled=True)  21.3 us
    all_to_all x1, blocking collectives, local(): parts = lax.all_to_all(parts, ('band_hi', 'band_lo'), 0, 0, tiled=True)  18.8 us
    pallas_call x1, Pallas kernels, run_forward(): pl.pallas_call(forward_kernel, grid=(HALF // CB,), out_shape=(jax.ShapeDt...  15.3 us
    pallas_call x1, Pallas kernels, run_gradient(): pl.pallas_call(gradient_kernel, out_shape=jax.ShapeDtypeStruct((8, PART,...  7.27 us
    pallas_call x1, Pallas kernels, run_focal(): pl.pallas_call(focal_kernel, out_shape=jax.ShapeDtypeStruct((PAIR * 16, W...  2.42 us
    unnamed x12, local copies, waits for them, and re-layouts  2.21 us
    ppermute x1, starting transfers between devices, local(): lax.ppermute(level, 'band_lo', [(0, 1), (1, 0)])  2.13 us
  transfers between devices with their start and end apart: 1, of which 0 were waited for; matrix products, arithmetic and copies ran while one was open for 0% of the time, Pallas kernels for 16%

profile of v5, /device:TPU:1, one launch (start us, length us, event | category | flops | bytes accessed | tf_op | source)
XLA Modules:
  0.0 96.1 jit_solution(16030776607577755669)
XLA Ops:
  0.0 0.0 copy-start.5
  0.0 0.0 copy-start.4
  0.0 2.1 %collective-permute-start = (s32[2]{0:T(128)}, s32[2]{0:T(128)S(1)}, u32[]{:S(2)}, u32[]{:S(2)}) collective-permute-start(s32[2]{0:T(128)} %level.1), channel_id=1, source_target_pairs={{0,16},{16,0},{1,17},{17,1},{2,18},{18,2},{3,19},{19,3},{4,20},{20... | collective-permute-start | bytes 32 | tf_op jit(solution)/shard_map/ppermute | solution.py:388
  2.1 15.3 %forward.1 = (bf16[2,2,256,2048]{3,2,1,0:T(8,128)(2,1)}, bf16[2,2,256,2048]{3,2,1,0:T(8,128)(2,1)}, f32[4,128,2048]{2,1,0:T(8,128)}, bf16[16,128,256]{2,1,0:T(8,128)(2,1)}) custom-call(s32[2]{0:T(128)} %level.1, f32[256,4096]{1,0:T(8,128)} %ph_l.1, f32[256,4096]{1,0:T(8,128)} %ph_l.1, s32[256,4096]{1,0:T(8,128)} %ap_l.1, s32[256,4096]{1,0:T(8,128)} %ap_l.1), custom_call_target="tpu_custom_call" | custom-call | tf_op jit(solution)/shard_map/forward/pallas_call | solution.py:328
  17.5 0.0 collective-permute-done
  17.5 0.0 copy-done.5
  17.5 0.1 pad_add_fusion.level
  17.6 25.5 %all_to_all.15.x = bf16[16,128,256]{2,1,0:T(8,128)(2,1)S(1)} all-to-all(bf16[16,128,256]{2,1,0:T(8,128)(2,1)} %get-tuple-element.13), channel_id=1, replica_groups=mesh['band_hi'=4,'band_lo'=2,'row'=16] {'row'}, dimensions={0} | all-to-all | bytes 2097152 | tf_op jit(solution)/shard_map/all_to_all | solution.py:391
  43.1 0.0 copy-done.4
  43.1 0.0 copy-start
  43.1 2.2 %copy-done = bf16[2,2,256,2048]{3,2,1,0:T(8,128)(2,1)S(1)} copy-done((bf16[2,2,256,2048]{3,2,1,0:T(8,128)(2,1)S(1)}, bf16[2,2,256,2048]{3,2,1,0:T(8,128)(2,1)}, u32[]{:S(2)}) %copy-start) | copy-done | bytes 4194328
  45.3 0.0 copy-start.1
  45.3 0.0 copy-start.2
  45.3 0.0 copy-start.3
  45.3 2.4 %focal.1 = bf16[32,128,128]{2,1,0:T(8,128)(2,1)S(1)} custom-call(bf16[16,128,256]{2,1,0:T(8,128)(2,1)S(1)} %all_to_all.15.x, bf16[2,2,256,2048]{3,2,1,0:T(8,128)(2,1)S(1)} %copy-done, f32[2,32,512]{2,1,0:T(8,128)S(1)} %copy-done.4), custom_call_target="tpu_custom_call" | custom-call | flops 17179869184 | bytes 67108864 | tf_op jit(solution)/shard_map/focal/pallas_call | solution.py:356
  47.7 21.3 %all_to_all.16.x = bf16[32,128,128]{2,1,0:T(8,128)(2,1)S(1)} all-to-all(bf16[32,128,128]{2,1,0:T(8,128)(2,1)S(1)} %focal.1), channel_id=1, replica_groups=mesh['band_hi'=4,'band_lo'=2,'row'=16] {'band_lo','row'}, dimensions={0} | all-to-all | bytes 2097152 | tf_op jit(solution)/shard_map/all_to_all | solution.py:393
  69.0 0.0 copy-done.1
  69.0 0.0 copy-done.2
  69.0 0.0 copy-done.3
  69.0 7.3 %gradient.1 = bf16[8,128,512]{2,1,0:T(8,128)(2,1)S(1)} custom-call(s32[4]{0:T(128)S(1)} %pad_add_fusion.level, bf16[32,128,128]{2,1,0:T(8,128)(2,1)S(1)} %all_to_all.16.x, bf16[2,2,256,2048]{3,2,1,0:T(8,128)(2,1)S(1)} %copy-done.1, bf16[2,2,256,2048]{3,2,1,0:T(8,128)(2,1)S(1)} %copy-done.2, f32[4,128,2048]{2,1,0:T(8,128)S(1)} %copy-done.3), custom_call_target="tpu_custom_call" | custom-call | flops 17179869184 | bytes 67108864 | tf_op jit(solution)/shard_map/gradient/pallas_call | solution.py:369
  76.3 18.8 %all_to_all.17 = bf16[8,128,512]{2,1,0:T(8,128)(2,1)S(1)} all-to-all(bf16[8,128,512]{2,1,0:T(8,128)(2,1)S(1)} %gradient.1), channel_id=1, replica_groups=mesh['band_hi'=4,'band_lo'=2,'row'=16] {'band_hi','band_lo'}, dimensions={0} | all-to-all | bytes 2097152 | tf_op jit(solution)/shard_map/all_to_all | solution.py:395
  95.1 0.9 convert_reduce_fusion
Async XLA Ops:
  0.0 17.5 %copy-start.5 = (s32[2]{0:T(128)S(1)}, s32[2]{0:T(128)}, u32[]{:S(2)}) copy-start(s32[2]{0:T(128)} %level.1) | copy-start | bytes 28
  0.0 43.1 %copy-start.4 = (f32[2,32,512]{2,1,0:T(8,128)S(1)}, f32[2,32,512]{2,1,0:T(8,128)}, u32[]{:S(2)}) copy-start(f32[2,32,512]{2,1,0:T(8,128)} %seen.1) | copy-start | bytes 393220
  0.0 17.5 %collective-permute-start = (s32[2]{0:T(128)}, s32[2]{0:T(128)S(1)}, u32[]{:S(2)}, u32[]{:S(2)}) collective-permute-start(s32[2]{0:T(128)} %level.1), channel_id=1, source_target_pairs={{0,16},{16,0},{1,17},{17,1},{2,18},{18,2},{3,19},{19,3},{4,20},{20... | collective-permute-start | bytes 32 | tf_op jit(solution)/shard_map/ppermute | solution.py:388
  43.1 2.2 %copy-start = (bf16[2,2,256,2048]{3,2,1,0:T(8,128)(2,1)S(1)}, bf16[2,2,256,2048]{3,2,1,0:T(8,128)(2,1)}, u32[]{:S(2)}) copy-start(bf16[2,2,256,2048]{3,2,1,0:T(8,128)(2,1)} %get-tuple-element.14.tab) | copy-start | bytes 12582916
  45.3 23.7 %copy-start.1 = (bf16[2,2,256,2048]{3,2,1,0:T(8,128)(2,1)S(1)}, bf16[2,2,256,2048]{3,2,1,0:T(8,128)(2,1)}, u32[]{:S(2)}) copy-start(bf16[2,2,256,2048]{3,2,1,0:T(8,128)(2,1)} %get-tuple-element.14.tab) | copy-start | bytes 12582916
  45.3 23.7 %copy-start.2 = (bf16[2,2,256,2048]{3,2,1,0:T(8,128)(2,1)S(1)}, bf16[2,2,256,2048]{3,2,1,0:T(8,128)(2,1)}, u32[]{:S(2)}) copy-start(bf16[2,2,256,2048]{3,2,1,0:T(8,128)(2,1)} %get-tuple-element.15.tab2) | copy-start | bytes 12582916
  45.3 23.7 %copy-start.3 = (f32[4,128,2048]{2,1,0:T(8,128)S(1)}, f32[4,128,2048]{2,1,0:T(8,128)}, u32[]{:S(2)}) copy-start(f32[4,128,2048]{2,1,0:T(8,128)} %get-tuple-element.16.fld) | copy-start | bytes 12582916

commit v6 on v5

--- a/solution.py
+++ b/solution.py
@@ -18,6 +18,10 @@
 BLK = 256
 CB = 512
 SUB = 256
+FWD_VMEM = 57
+SIDE_VMEM = 57
+STEP = 256
+DOT = 512
 CHUNK = 32
 STEPS = HALF // BLK
 WL = 2
@@ -105,7 +109,7 @@
     return jnp.where(jnp.where(flip, size - 1 - c, c) == r, 1.0, 0.0).astype(BF16)
 
 
-def write_tables(tab, first, wave0):
+def write_tables(tab, first, wave0, place):
     k = lax.broadcasted_iota(jnp.int32, (8, 128), 0) + 1
     lane = lax.broadcasted_iota(jnp.int32, (8, 128), 1)
     at, state = [], []
@@ -115,88 +119,124 @@
             x = 2 * (first + t + lane) + 1
             c, s = angle((x * k).astype(F32), m)
             rc, rs = angle((x * 8).astype(F32), m)
-            at.append((w, t))
+            at.append((w, pl.ds(pl.multiple_of(place + t, 128), 128)))
             state.append((c * NORM, s * NORM, rc, rs))
     for q in range(K // 16):
-        for n, (w, t) in enumerate(at):
+        rows = slice(16 * q, 16 * q + 16)
+        for n, (w, lanes) in enumerate(at):
             c0, s0, rc, rs = state[n]
             c1, s1 = c0 * rc - s0 * rs, c0 * rs + s0 * rc
-            rows, lanes = slice(16 * q, 16 * q + 16), slice(t, t + 128)
             tab[w, 0, rows, lanes] = jnp.concatenate([c0, c1], axis=0).astype(BF16)
             tab[w, 1, rows, lanes] = jnp.concatenate([s0, s1], axis=0).astype(BF16)
             state[n] = (c1 * rc - s1 * rs, c1 * rs + s1 * rc, rc, rs)
 
 
-def forward_kernel(level, ph_r, ph_l, ap_r, ap_l, tab, tab2, fld, out, *scratch):
-    n_sub = CB // SUB
-    e_all, o_all = scratch[:n_sub], scratch[n_sub : 2 * n_sub]
-    xacc, yacc, tmp = scratch[2 * n_sub :]
+def forward_kernel(level, ph_in, ap_in, out, *scratch):
+    e_s, o_s, ph, ap, tab, xacc, yacc, tmp, sem_in = scratch
+    row = lax.axis_index("row")
+    blocks = HALF // CB
+
+    def right(i):
+        return pl.ds(pl.multiple_of(HALF + i * CB, CB), CB)
+
+    def left(i):
+        return pl.ds(pl.multiple_of(HALF - CB - i * CB, CB), CB)
+
+    def fetch(i):
+        return [
+            pltpu.make_async_copy(src.at[:, cols], dst.at[:, cols], sem_in.at[i, n])
+            for n, (src, dst, cols) in enumerate(
+                ((ph_in, ph, right(i)), (ph_in, ph, left(i)), (ap_in, ap, right(i)), (ap_in, ap, left(i)))
+            )
+        ]
+
+    for i in range(blocks):
+        for copy in fetch(i):
+            copy.start()
+    ones = jnp.full((16, HALF), NORM, BF16)
+
+    def block(i, _):
+        base = pl.multiple_of(i * CB, CB)
+        cols = pl.ds(base, CB)
+
+        def tables(n, _):
+            write_tables(tab, base, 0, base)
+            return 0
+
+        lax.fori_loop(0, jnp.minimum(i + 1, 1), tables, 0)
+        for copy in fetch(i):
+            copy.wait()
+        dx = [chirp_cols(level[w], base, CB) for w in range(WL)]
+
+        def rows(t, _):
+            for r1 in range(0, STEP, CHUNK):
+                for h in range(0, CB, SUB):
+                    sl = pl.ds(pl.multiple_of(t * STEP + r1, CHUNK), CHUNK)
+                    here = slice(h, h + SUB)
+                    there = pl.ds(pl.multiple_of(base + h, SUB), SUB)
+                    straight = pl.ds(pl.multiple_of(HALF + base + h, SUB), SUB)
+                    mirror = pl.ds(pl.multiple_of(HALF - SUB - base - h, SUB), SUB)
+                    fr_c, fr_s = field(ph[sl, straight], ap[sl, straight].astype(F32))
+                    fl_c, fl_s = field(lane_rev(ph[sl, mirror]), lane_rev(ap[sl, mirror]).astype(F32))
+                    ec, es = fr_c + fl_c, fr_s + fl_s
+                    oc, os = fr_c - fl_c, fr_s - fl_s
+                    for w in range(WL):
+                        dc, ds = dx[w][0][:, here], dx[w][1][:, here]
+                        e_s[w, 0, sl, there] = (ec * dc - es * ds).astype(BF16)
+                        e_s[w, 1, sl, there] = (ec * ds + es * dc).astype(BF16)
+                        o_s[w, 0, sl, there] = (oc * dc - os * ds).astype(BF16)
+                        o_s[w, 1, sl, there] = (oc * ds + os * dc).astype(BF16)
+            return 0
+
+        lax.fori_loop(0, ROWS // STEP, rows, 0)
+
+        return 0
+
+    lax.fori_loop(0, blocks, block, 0)
+    def dots(w, _):
+        c = jnp.concatenate([tab[w, 0], ones], axis=0)
+        s = tab[w, 1]
+        for part in range(2):
+            xacc[w, part] = nt(c, e_s[w, part])
+            yacc[w, part] = nt(s, o_s[w, part])
+        return 0
+
+    lax.fori_loop(0, WL, dots, 0)
+    j = flip_matrix(row < 8, ROWS)
+    pos = row * ROWS + lax.broadcasted_iota(jnp.int32, (1, ROWS), 1)
+    for w in range(WL):
+        dc, ds = chirp_rows(level[w], pos)
+        xr, xi = xacc[w, 0], xacc[w, 1]
+        yr, yi = yacc[w, 0], yacc[w, 1]
+        xr, xi = xr * dc - xi * ds, xr * ds + xi * dc
+        yr, yi = yr * dc - yi * ds, yr * ds + yi * dc
+        x0 = (xr[K : K + 1], xi[K : K + 1])
+        xr, xi = xr[:K], xi[:K]
+        plus = (xr + yi, xi - yr)
+        minus = (xr - yi, xi + yr)
+        for part in range(2):
+            tmp[pl.ds(8, K), :] = plus[part]
+            tmp[pl.ds(7, 1), :] = x0[part]
+            p = nn(tmp[pl.ds(7, K), :].astype(BF16), j).astype(BF16)
+            m = nn(minus[part].astype(BF16), j).astype(BF16)
+            at = (w * 2 + part) * GRP
+            for g in range(8):
+                out[8 + g, at : at + GRP, :] = p[g * GRP : (g + 1) * GRP]
+                out[7 - g, at : at + GRP, :] = m[g * GRP : (g + 1) * GRP]
+
+
+def side_kernel(ph_r, ph_l, ap_r, ap_l, tab, tab2, fld):
     i = pl.program_id(0)
-    row = lax.axis_index("row")
-    mine = lax.axis_index("band_lo") * PART
-
-    @pl.when(i == 0)
-    def _():
-        xacc[...] = jnp.zeros_like(xacc)
-        yacc[...] = jnp.zeros_like(yacc)
-
-    write_tables(tab, i * CB, 0)
-    write_tables(tab2, i * CB, WL)
-    dx = [chirp_cols(level[w], i * CB, CB) for w in range(WL)]
-    ones = jnp.full((16, SUB), NORM, BF16)
-    for n in range(n_sub):
-        h = n * SUB
-        e_s, o_s = e_all[n], o_all[n]
-        cols = slice(h, h + SUB)
-        mirror = slice(CB - SUB - h, CB - h)
-        for r0 in range(0, ROWS, CHUNK):
-            sl = pl.ds(pl.multiple_of((mine + r0) % ROWS, CHUNK), CHUNK)
-            fr_c, fr_s = field(ph_r[sl, cols], ap_r[sl, cols].astype(F32))
-            fl_c, fl_s = field(lane_rev(ph_l[sl, mirror]), lane_rev(ap_l[sl, mirror]).astype(F32))
-            if r0 < PART:
-                keep = slice(r0, r0 + CHUNK)
-                fld[0, keep, cols] = fr_c
-                fld[1, keep, cols] = fr_s
-                fld[2, keep, cols] = fl_c
-                fld[3, keep, cols] = fl_s
-            ec, es = fr_c + fl_c, fr_s + fl_s
-            oc, os = fr_c - fl_c, fr_s - fl_s
-            for w in range(WL):
-                dc, ds = dx[w][0][:, cols], dx[w][1][:, cols]
-                e_s[w, 0, sl, :] = (ec * dc - es * ds).astype(BF16)
-                e_s[w, 1, sl, :] = (ec * ds + es * dc).astype(BF16)
-                o_s[w, 0, sl, :] = (oc * dc - os * ds).astype(BF16)
-                o_s[w, 1, sl, :] = (oc * ds + os * dc).astype(BF16)
-        for w in range(WL):
-            c = jnp.concatenate([tab[w, 0, :, cols], ones], axis=0)
-            s = tab[w, 1, :, cols]
-            for part in range(2):
-                xacc[w, part] += nt(c, e_s[w, part])
-                yacc[w, part] += nt(s, o_s[w, part])
-
-    @pl.when(i == HALF // CB - 1)
-    def _():
-        j = flip_matrix(row < 8, ROWS)
-        pos = row * ROWS + lax.broadcasted_iota(jnp.int32, (1, ROWS), 1)
-        for w in range(WL):
-            dc, ds = chirp_rows(level[w], pos)
-            xr, xi = xacc[w, 0], xacc[w, 1]
-            yr, yi = yacc[w, 0], yacc[w, 1]
-            xr, xi = xr * dc - xi * ds, xr * ds + xi * dc
-            yr, yi = yr * dc - yi * ds, yr * ds + yi * dc
-            x0 = (xr[K : K + 1], xi[K : K + 1])
-            xr, xi = xr[:K], xi[:K]
-            plus = (xr + yi, xi - yr)
-            minus = (xr - yi, xi + yr)
-            for part in range(2):
-                tmp[pl.ds(8, K), :] = plus[part]
-                tmp[pl.ds(7, 1), :] = x0[part]
-                p = nn(tmp[pl.ds(7, K), :].astype(BF16), j).astype(BF16)
-                m = nn(minus[part].astype(BF16), j).astype(BF16)
-                at = (w * 2 + part) * GRP
-                for g in range(8):
-                    out[8 + g, at : at + GRP, :] = p[g * GRP : (g + 1) * GRP]
-                    out[7 - g, at : at + GRP, :] = m[g * GRP : (g + 1) * GRP]
+    write_tables(tab, i * CB, 0, 0)
+    write_tables(tab2, i * CB, WL, 0)
+
+    def rows(t, _):
+        sl = pl.ds(pl.multiple_of(t * CHUNK, CHUNK), CHUNK)
+        fld[0, sl, :], fld[1, sl, :] = field(ph_r[sl, :], ap_r[sl, :].astype(F32))
+        fld[2, sl, :], fld[3, sl, :] = field(lane_rev(ph_l[sl, :]), lane_rev(ap_l[sl, :]).astype(F32))
+        return 0
+
+    lax.fori_loop(0, PART // CHUNK, rows, 0)
 
 
 def focal_kernel(x, tab, seen, out, obs):
@@ -322,34 +362,48 @@
 
 
 def run_forward(level, phase, aperture):
-    smem = pl.BlockSpec(memory_space=pltpu.SMEM)
-    right = pl.BlockSpec((ROWS, CB), lambda i: (0, HALF // CB + i))
-    left = pl.BlockSpec((ROWS, CB), lambda i: (0, HALF // CB - 1 - i))
+    any_space = pl.BlockSpec(memory_space=pl.ANY)
     return pl.pallas_call(
         forward_kernel,
+        out_shape=jax.ShapeDtypeStruct((16, WL * 2 * GRP, ROWS), BF16),
+        in_specs=[pl.BlockSpec(memory_space=pltpu.SMEM), any_space, any_space],
+        out_specs=pl.BlockSpec(memory_space=pltpu.VMEM),
+        scratch_shapes=[pltpu.VMEM((WL, 2, ROWS, HALF), BF16)] * 2
+        + [
+            pltpu.VMEM((ROWS, N), F32),
+            pltpu.VMEM((ROWS, N), jnp.int32),
+            pltpu.VMEM((WL, 2, K, HALF), BF16),
+            pltpu.VMEM((WL, 2, K + 16, ROWS), F32),
+            pltpu.VMEM((WL, 2, K, ROWS), F32),
+            pltpu.VMEM((K + 16, ROWS), F32),
+            pltpu.SemaphoreType.DMA((HALF // CB, 4)),
+        ],
+        compiler_params=pltpu.CompilerParams(vmem_limit_bytes=FWD_VMEM * 2**20),
+        name="forward",
+    )(level, phase, aperture)
+
+
+def run_side(phase, aperture):
+    right = pl.BlockSpec((PART, CB), lambda i: (0, HALF // CB + i))
+    left = pl.BlockSpec((PART, CB), lambda i: (0, HALF // CB - 1 - i))
+    return pl.pallas_call(
+        side_kernel,
         grid=(HALF // CB,),
         out_shape=(
             jax.ShapeDtypeStruct((WL, 2, K, HALF), BF16),
             jax.ShapeDtypeStruct((WL, 2, K, HALF), BF16),
             jax.ShapeDtypeStruct((4, PART, HALF), F32),
-            jax.ShapeDtypeStruct((16, WL * 2 * GRP, ROWS), BF16),
         ),
-        in_specs=[smem, right, left, right, left],
+        in_specs=[right, left, right, left],
         out_specs=(
             pl.BlockSpec((WL, 2, K, CB), lambda i: (0, 0, 0, i)),
             pl.BlockSpec((WL, 2, K, CB), lambda i: (0, 0, 0, i)),
             pl.BlockSpec((4, PART, CB), lambda i: (0, 0, i)),
-            pl.BlockSpec((16, WL * 2 * GRP, ROWS), lambda i: (0, 0, 0)),
         ),
-        scratch_shapes=[pltpu.VMEM((WL, 2, ROWS, SUB), BF16)] * (2 * CB // SUB)
-        + [
-            pltpu.VMEM((WL, 2, K + 16, ROWS), F32),
-            pltpu.VMEM((WL, 2, K, ROWS), F32),
-            pltpu.VMEM((K + 16, ROWS), F32),
-        ],
-        compiler_params=pltpu.CompilerParams(vmem_limit_bytes=60 * 2**20),
-        name="forward",
-    )(level, phase, phase, aperture, aperture)
+        compiler_params=pltpu.CompilerParams(vmem_limit_bytes=SIDE_VMEM * 2**20),
+        cost_estimate=pl.CostEstimate(flops=2**32, bytes_accessed=2**24, transcendentals=0),
+        name="side",
+    )(phase, phase, aperture, aperture)
 
 
 def run_focal(x, tab, seen):
@@ -386,9 +440,14 @@
 def local(phase, aperture, defocus_index, intensity):
     level = defocus_index.astype(jnp.int32)
     levels = jnp.concatenate([level, lax.ppermute(level, "band_lo", [(0, 1), (1, 0)])])
-    tab, tab2, fld, sent = run_forward(level, phase, aperture)
-    sent, levels = lax.optimization_barrier((sent, levels))
+    sent = run_forward(level, phase, aperture)
+    sent, levels, phase, aperture = lax.optimization_barrier((sent, levels, phase, aperture))
     got = lax.all_to_all(sent, "row", 0, 0, tiled=True)
+    mine = lax.axis_index("band_lo") * PART
+    tab, tab2, fld = run_side(
+        lax.dynamic_slice_in_dim(phase, mine, PART, 0), lax.dynamic_slice_in_dim(aperture, mine, PART, 0)
+    )
+    got, tab, tab2, fld = lax.optimization_barrier((got, tab, tab2, fld))
     sent = run_focal(got, tab, intensity)
     got = lax.all_to_all(sent, ("band_lo", "row"), 0, 0, tiled=True)
     parts = run_gradient(levels, got, tab, tab2, fld)

time: 96.3 us -> 95.2 us (0.989)
  blocking collectives: 65.7 us -> 40.1 us
  starting transfers between devices: 2.13 us -> 10.7 us
  Pallas kernels: 25 us -> 32.8 us
  local copies, waits for them, and re-layouts: 2.21 us -> 6.93 us
  waiting for transfers between devices: 0.01 us -> 3.26 us
    all_to_all x1 -> x0, blocking collectives: 25.5 us -> none  [local(): got = lax.all_to_all(sent, 'row', 0, 0, tiled=True)]
    all_to_all x0 -> x1, starting transfers between devices: none -> 8.62 us  [local(): got = lax.all_to_all(sent, 'row', 0, 0, tiled=True)]
    pallas_call x1 -> x2, Pallas kernels: 15.3 us -> 23.1 us  [the longest x1 13.9 us: run_forward(): pl.pallas_call(forward_kernel, out_shape=jax.ShapeDtypeStruct((16, WL * 2...]
    dynamic_slice x0 -> x2, local copies, waits for them, and re-layouts: none -> 4.72 us  [the longest x1 3.27 us: local(): lax.dynamic_slice_in_dim(phase, mine, PART, 0)]
    all_to_all x0 -> x1, waiting for transfers between devices: none -> 3.26 us  [local(): got = lax.all_to_all(sent, 'row', 0, 0, tiled=True)]
    unnamed x12 -> x14, local copies, waits for them, and re-layouts: 2.21 us -> 2.21 us
  transfers between devices with their start and end apart: 1 -> 2, of which waited for: 0 -> 1; matrix products, arithmetic and copies ran while one was open for 0% -> 5% of each run, Pallas kernels for 16% -> 24%
where the time goes in v6:
time: 95.2 us; the launch traced here: 94.8 us
  blocking collectives  40.1 us (42%)
  Pallas kernels  32.8 us (34%)
  starting transfers between devices  10.7 us (11%)
  local copies, waits for them, and re-layouts  6.93 us (7%)
  waiting for transfers between devices  3.26 us (3%)
  other arithmetic  1.01 us (1%)
    all_to_all x1, blocking collectives, local(): got = lax.all_to_all(sent, ('band_lo', 'row'), 0, 0, tiled=True)  21.2 us
    all_to_all x1, blocking collectives, local(): parts = lax.all_to_all(parts, ('band_hi', 'band_lo'), 0, 0, tiled=True)  18.8 us
    pallas_call x1, Pallas kernels, run_forward(): pl.pallas_call(forward_kernel, out_shape=jax.ShapeDtypeStruct((16, WL * 2...  13.9 us
    pallas_call x1, Pallas kernels, run_side(): pl.pallas_call(side_kernel, grid=(HALF // CB,), out_shape=(jax.ShapeDtype...  9.21 us
    all_to_all x1, starting transfers between devices, local(): got = lax.all_to_all(sent, 'row', 0, 0, tiled=True)  8.62 us
    pallas_call x1, Pallas kernels, run_gradient(): pl.pallas_call(gradient_kernel, out_shape=jax.ShapeDtypeStruct((8, PART,...  7.26 us
    dynamic_slice x1, local copies, waits for them, and re-layouts, local(): lax.dynamic_slice_in_dim(phase, mine, PART, 0)  3.27 us
    all_to_all x1, waiting for transfers between devices, local(): got = lax.all_to_all(sent, 'row', 0, 0, tiled=True)  3.26 us
  transfers between devices with their start and end apart: 2, of which 1 were waited for; matrix products, arithmetic and copies ran while one was open for 5% of the time, Pallas kernels for 24%

profile of v6, /device:TPU:1, one launch (start us, length us, event | category | flops | bytes accessed | tf_op | source)
XLA Modules:
  0.0 94.8 jit_solution(189348558878616455)
XLA Ops:
  0.0 2.1 %collective-permute-start = (s32[2]{0:T(128)}, s32[2]{0:T(128)S(1)}, u32[]{:S(2)}, u32[]{:S(2)}) collective-permute-start(s32[2]{0:T(128)} %level.1), channel_id=1, source_target_pairs={{0,16},{16,0},{1,17},{17,1},{2,18},{18,2},{3,19},{19,3},{4,20},{20... | collective-permute-start | bytes 32 | tf_op jit(solution)/shard_map/ppermute | solution.py:442
  2.1 0.0 copy-start.6
  2.1 13.9 %forward.1 = bf16[16,128,256]{2,1,0:T(8,128)(2,1)} custom-call(s32[2]{0:T(128)} %level.1, f32[256,4096]{1,0:T(8,128)} %ph_in.1, s32[256,4096]{1,0:T(8,128)} %ap_in.1), custom_call_target="tpu_custom_call" | custom-call | tf_op jit(solution)/shard_map/forward/pallas_call | solution.py:366
  16.0 0.0 collective-permute-done
  16.0 0.0 copy-done.6
  16.0 0.1 pad_add_fusion.level
  16.1 8.6 %all-to-all-start = ((bf16[16,128,256]{2,1,0:T(8,128)(2,1)}), bf16[16,128,256]{2,1,0:T(8,128)(2,1)S(1)}, u32[]{:S(2)}, u32[]{:S(2)}) async-start(bf16[16,128,256]{2,1,0:T(8,128)(2,1)} %forward.1), calls=%async_computation | async-start | bytes 2097152 | tf_op jit(solution)/shard_map/all_to_all | solution.py:445
  24.7 0.0 copy-start.5
  24.7 3.3 %constant_dynamic-slice_fusion.1.ph_r.ph_l = f32[128,4096]{1,0:T(8,128)} fusion(f32[256,4096]{1,0:T(8,128)} %ph_in.1, s32[]{:T(128)S(6)} %select_n.4), kind=kLoop, calls=%fused_computation.3 | loop fusion | bytes 4194308 | tf_op jit(solution)/shard_map/dynamic_slice | solution.py:448
  28.0 0.0 copy-done.5
  28.0 1.4 %constant_dynamic-slice_fusion.ap_r.ap_l = s32[128,4096]{1,0:T(8,128)} fusion(s32[256,4096]{1,0:T(8,128)S(1)} %copy-done.5, s32[]{:T(128)S(6)} %select_n.4), kind=kLoop, calls=%fused_computation.2 | loop fusion | bytes 4194308 | tf_op jit(solution)/shard_map/dynamic_slice | solution.py:448
  29.4 0.0 copy-start
  29.5 9.2 %side.1 = (bf16[2,2,256,2048]{3,2,1,0:T(8,128)(2,1)}, bf16[2,2,256,2048]{3,2,1,0:T(8,128)(2,1)}, f32[4,128,2048]{2,1,0:T(8,128)}) custom-call(f32[128,4096]{1,0:T(8,128)} %constant_dynamic-slice_fusion.1.ph_r.ph_l, f32[128,4096]{1,0:T(8,128)} %constant_dynamic-slice_fusion.1.ph_r.ph_l, s32[128,4096]{1,0:T(8,128)} %constant_dynamic-slice_fusion.ap_r.ap_l, ...), custom_call_target="tpu_custom_call" | custom-call | flops 4294967296 | bytes 16777216 | tf_op jit(solution)/shard_map/side/pallas_call | solution.py:389
  38.7 3.3 %all-to-all-done.x = bf16[16,128,256]{2,1,0:T(8,128)(2,1)S(1)} async-done(((bf16[16,128,256]{2,1,0:T(8,128)(2,1)}), bf16[16,128,256]{2,1,0:T(8,128)(2,1)S(1)}, u32[]{:S(2)}, u32[]{:S(2)}) %all-to-all-start) | async-done | bytes 1048608 | tf_op jit(solution)/shard_map/all_to_all | solution.py:445
  41.9 0.0 copy-done
  41.9 0.0 copy-start.1
  41.9 2.2 %copy-done.1 = bf16[2,2,256,2048]{3,2,1,0:T(8,128)(2,1)S(1)} copy-done((bf16[2,2,256,2048]{3,2,1,0:T(8,128)(2,1)S(1)}, bf16[2,2,256,2048]{3,2,1,0:T(8,128)(2,1)}, u32[]{:S(2)}) %copy-start.1) | copy-done | bytes 4194328
  44.1 0.0 copy-start.2
  44.1 0.0 copy-start.3
  44.1 0.0 copy-start.4
  44.1 2.4 %focal.1 = bf16[32,128,128]{2,1,0:T(8,128)(2,1)S(1)} custom-call(bf16[16,128,256]{2,1,0:T(8,128)(2,1)S(1)} %all-to-all-done.x, bf16[2,2,256,2048]{3,2,1,0:T(8,128)(2,1)S(1)} %copy-done.1, f32[2,32,512]{2,1,0:T(8,128)S(1)} %copy-done), custom_call_target="tpu_custom_call" | custom-call | flops 17179869184 | bytes 67108864 | tf_op jit(solution)/shard_map/focal/pallas_call | solution.py:410
  46.6 21.2 %all_to_all.15.x = bf16[32,128,128]{2,1,0:T(8,128)(2,1)S(1)} all-to-all(bf16[32,128,128]{2,1,0:T(8,128)(2,1)S(1)} %focal.1), channel_id=1, replica_groups=mesh['band_hi'=4,'band_lo'=2,'row'=16] {'band_lo','row'}, dimensions={0} | all-to-all | bytes 2097152 | tf_op jit(solution)/shard_map/all_to_all | solution.py:452
  67.8 0.0 copy-done.2
  67.8 0.0 copy-done.3
  67.8 0.0 copy-done.4
  67.8 7.3 %gradient.1 = bf16[8,128,512]{2,1,0:T(8,128)(2,1)S(1)} custom-call(s32[4]{0:T(128)S(1)} %pad_add_fusion.level, bf16[32,128,128]{2,1,0:T(8,128)(2,1)S(1)} %all_to_all.15.x, bf16[2,2,256,2048]{3,2,1,0:T(8,128)(2,1)S(1)} %copy-done.2, bf16[2,2,256,2048]{3,2,1,0:T(8,128)(2,1)S(1)} %copy-done.3, f32[4,128,2048]{2,1,0:T(8,128)S(1)} %copy-done.4), custom_call_target="tpu_custom_call" | custom-call | flops 17179869184 | bytes 67108864 | tf_op jit(solution)/shard_map/gradient/pallas_call | solution.py:423
  75.1 18.8 %all_to_all.16 = bf16[8,128,512]{2,1,0:T(8,128)(2,1)S(1)} all-to-all(bf16[8,128,512]{2,1,0:T(8,128)(2,1)S(1)} %gradient.1), channel_id=1, replica_groups=mesh['band_hi'=4,'band_lo'=2,'row'=16] {'band_hi','band_lo'}, dimensions={0} | all-to-all | bytes 2097152 | tf_op jit(solution)/shard_map/all_to_all | solution.py:454
  93.9 0.9 convert_reduce_fusion
Async XLA Ops:
  0.0 16.0 %collective-permute-start = (s32[2]{0:T(128)}, s32[2]{0:T(128)S(1)}, u32[]{:S(2)}, u32[]{:S(2)}) collective-permute-start(s32[2]{0:T(128)} %level.1), channel_id=1, source_target_pairs={{0,16},{16,0},{1,17},{17,1},{2,18},{18,2},{3,19},{19,3},{4,20},{20... | collective-permute-start | bytes 32 | tf_op jit(solution)/shard_map/ppermute | solution.py:442
  2.1 13.9 %copy-start.6 = (s32[2]{0:T(128)S(1)}, s32[2]{0:T(128)}, u32[]{:S(2)}) copy-start(s32[2]{0:T(128)} %level.1) | copy-start | bytes 28
  16.1 25.8 %all-to-all-start = ((bf16[16,128,256]{2,1,0:T(8,128)(2,1)}), bf16[16,128,256]{2,1,0:T(8,128)(2,1)S(1)}, u32[]{:S(2)}, u32[]{:S(2)}) async-start(bf16[16,128,256]{2,1,0:T(8,128)(2,1)} %forward.1), calls=%async_computation | async-start | bytes 2097152 | tf_op jit(solution)/shard_map/all_to_all | solution.py:445
  24.7 3.3 %copy-start.5 = (s32[256,4096]{1,0:T(8,128)S(1)}, s32[256,4096]{1,0:T(8,128)}, u32[]{:S(2)}) copy-start(s32[256,4096]{1,0:T(8,128)} %ap_in.1) | copy-start | bytes 12582916
  29.4 12.5 %copy-start = (f32[2,32,512]{2,1,0:T(8,128)S(1)}, f32[2,32,512]{2,1,0:T(8,128)}, u32[]{:S(2)}) copy-start(f32[2,32,512]{2,1,0:T(8,128)} %seen.1) | copy-start | bytes 393220
  41.9 2.2 %copy-start.1 = (bf16[2,2,256,2048]{3,2,1,0:T(8,128)(2,1)S(1)}, bf16[2,2,256,2048]{3,2,1,0:T(8,128)(2,1)}, u32[]{:S(2)}) copy-start(bf16[2,2,256,2048]{3,2,1,0:T(8,128)(2,1)} %get-tuple-element.24.tab) | copy-start | bytes 12582916
  44.1 23.7 %copy-start.2 = (bf16[2,2,256,2048]{3,2,1,0:T(8,128)(2,1)S(1)}, bf16[2,2,256,2048]{3,2,1,0:T(8,128)(2,1)}, u32[]{:S(2)}) copy-start(bf16[2,2,256,2048]{3,2,1,0:T(8,128)(2,1)} %get-tuple-element.24.tab) | copy-start | bytes 12582916
  44.1 23.7 %copy-start.3 = (bf16[2,2,256,2048]{3,2,1,0:T(8,128)(2,1)S(1)}, bf16[2,2,256,2048]{3,2,1,0:T(8,128)(2,1)}, u32[]{:S(2)}) copy-start(bf16[2,2,256,2048]{3,2,1,0:T(8,128)(2,1)} %get-tuple-element.25.tab2) | copy-start | bytes 12582916
  44.1 23.7 %copy-start.4 = (f32[4,128,2048]{2,1,0:T(8,128)S(1)}, f32[4,128,2048]{2,1,0:T(8,128)}, u32[]{:S(2)}) copy-start(f32[4,128,2048]{2,1,0:T(8,128)} %get-tuple-element.26.fld) | copy-start | bytes 12582916

commit v7 on v6

--- a/solution.py
+++ b/solution.py
@@ -20,6 +20,7 @@
 SUB = 256
 FWD_VMEM = 57
 SIDE_VMEM = 57
+FAR = 8
 STEP = 256
 DOT = 512
 CHUNK = 32
@@ -225,9 +226,10 @@
                 out[7 - g, at : at + GRP, :] = m[g * GRP : (g + 1) * GRP]
 
 
-def side_kernel(ph_r, ph_l, ap_r, ap_l, tab, tab2, fld):
+def side_kernel(ph_r, ph_l, ap_r, ap_l, far, tab, tab2, fld):
     i = pl.program_id(0)
     write_tables(tab, i * CB, 0, 0)
+    far[...] = tab[...]
     write_tables(tab2, i * CB, WL, 0)
 
     def rows(t, _):
@@ -239,25 +241,34 @@
     lax.fori_loop(0, PART // CHUNK, rows, 0)
 
 
-def focal_kernel(x, tab, seen, out, obs):
+def focal_kernel(x, far, seen, out, obs, tab, sem):
+    fetch = []
+    for i in range(STEPS):
+        cols = slice(i * BLK, (i + 1) * BLK)
+        fetch.append(
+            pltpu.make_async_copy(far.at[:WL, :, :, cols], tab.at[:, :, :, cols], sem.at[i])
+        )
+        fetch[-1].start()
     low = lax.axis_index("row") < 8
     for w in range(WL):
         for r in range(GRP):
             obs[w, pl.ds(jnp.where(low, GRP - 1 - r, r), 1), :] = seen[w, r : r + 1, :]
     last = lax.broadcasted_iota(jnp.int32, (GRP, K), 1) == K - 1
-    for w in range(WL):
-        at = w * 2 * GRP
-        acc_c = jnp.zeros((2 * GRP, K), F32)
-        acc_s = jnp.zeros((2 * GRP, K), F32)
-        centre = jnp.zeros((2 * GRP, BLK), F32)
-        for i in range(STEPS):
+    acc = [[jnp.zeros((2 * GRP, K), F32)] * 2 + [jnp.zeros((2 * GRP, BLK), F32)] for w in range(WL)]
+    for i in range(STEPS):
+        fetch[i].wait()
+        cols = slice(i * BLK, (i + 1) * BLK)
+        for w in range(WL):
+            at = w * 2 * GRP
             r = x[8 + i, at : at + 2 * GRP, :].astype(F32)
             l = x[7 - i, at : at + 2 * GRP, :].astype(F32)
             e = r + l
-            centre = centre + e
-            cols = slice(i * BLK, (i + 1) * BLK)
-            acc_c = acc_c + nt(e.astype(BF16), tab[w, 0, :, cols])
-            acc_s = acc_s + nt((r - l).astype(BF16), tab[w, 1, :, cols])
+            acc[w][0] = acc[w][0] + nt(e.astype(BF16), tab[w, 0, :, cols])
+            acc[w][1] = acc[w][1] + nt((r - l).astype(BF16), tab[w, 1, :, cols])
+            acc[w][2] = acc[w][2] + e
+    for w in range(WL):
+        at = w * 2 * GRP
+        acc_c, acc_s, centre = acc[w]
         centre = jnp.sum(centre, axis=1, keepdims=True) * NORM
         cr, ci = acc_c[:GRP], acc_c[GRP:]
         sr, si = acc_s[:GRP], acc_s[GRP:]
@@ -384,12 +395,13 @@
 
 
 def run_side(phase, aperture):
-    right = pl.BlockSpec((PART, CB), lambda i: (0, HALF // CB + i))
-    left = pl.BlockSpec((PART, CB), lambda i: (0, HALF // CB - 1 - i))
+    right = pl.BlockSpec((PART, CB), lambda i: (lax.axis_index("band_lo"), HALF // CB + i))
+    left = pl.BlockSpec((PART, CB), lambda i: (lax.axis_index("band_lo"), HALF // CB - 1 - i))
     return pl.pallas_call(
         side_kernel,
         grid=(HALF // CB,),
         out_shape=(
+            jax.ShapeDtypeStruct((FAR * WL, 2, K, HALF), BF16),
             jax.ShapeDtypeStruct((WL, 2, K, HALF), BF16),
             jax.ShapeDtypeStruct((WL, 2, K, HALF), BF16),
             jax.ShapeDtypeStruct((4, PART, HALF), F32),
@@ -398,6 +410,7 @@
         out_specs=(
             pl.BlockSpec((WL, 2, K, CB), lambda i: (0, 0, 0, i)),
             pl.BlockSpec((WL, 2, K, CB), lambda i: (0, 0, 0, i)),
+            pl.BlockSpec((WL, 2, K, CB), lambda i: (0, 0, 0, i)),
             pl.BlockSpec((4, PART, CB), lambda i: (0, 0, i)),
         ),
         compiler_params=pltpu.CompilerParams(vmem_limit_bytes=SIDE_VMEM * 2**20),
@@ -410,10 +423,18 @@
     return pl.pallas_call(
         focal_kernel,
         out_shape=jax.ShapeDtypeStruct((PAIR * 16, WL * 2 * GRP, PART), BF16),
-        in_specs=[pl.BlockSpec(memory_space=pltpu.VMEM)] * 3,
+        in_specs=[
+            pl.BlockSpec(memory_space=pltpu.VMEM),
+            pl.BlockSpec(memory_space=pl.ANY),
+            pl.BlockSpec(memory_space=pltpu.VMEM),
+        ],
         out_specs=pl.BlockSpec(memory_space=pltpu.VMEM),
-        scratch_shapes=[pltpu.VMEM((WL, GRP, M), F32)],
-        compiler_params=pltpu.CompilerParams(vmem_limit_bytes=20 * 2**20),
+        scratch_shapes=[
+            pltpu.VMEM((WL, GRP, M), F32),
+            pltpu.VMEM((WL, 2, K, HALF), BF16),
+            pltpu.SemaphoreType.DMA((STEPS,)),
+        ],
+        compiler_params=pltpu.CompilerParams(vmem_limit_bytes=40 * 2**20),
         cost_estimate=pl.CostEstimate(flops=2**34, bytes_accessed=2**26, transcendentals=0),
         name="focal",
     )(x, tab, seen)
@@ -443,12 +464,9 @@
     sent = run_forward(level, phase, aperture)
     sent, levels, phase, aperture = lax.optimization_barrier((sent, levels, phase, aperture))
     got = lax.all_to_all(sent, "row", 0, 0, tiled=True)
-    mine = lax.axis_index("band_lo") * PART
-    tab, tab2, fld = run_side(
-        lax.dynamic_slice_in_dim(phase, mine, PART, 0), lax.dynamic_slice_in_dim(aperture, mine, PART, 0)
-    )
-    got, tab, tab2, fld = lax.optimization_barrier((got, tab, tab2, fld))
-    sent = run_focal(got, tab, intensity)
+    far, tab, tab2, fld = run_side(phase, aperture)
+    got, far, tab, tab2, fld = lax.optimization_barrier((got, far, tab, tab2, fld))
+    sent = run_focal(got, far, intensity)
     got = lax.all_to_all(sent, ("band_lo", "row"), 0, 0, tiled=True)
     parts = run_gradient(levels, got, tab, tab2, fld)
     parts = lax.all_to_all(parts, ("band_hi", "band_lo"), 0, 0, tiled=True)

time: 95.2 us -> 94.1 us (0.988)
  local copies, waits for them, and re-layouts: 6.93 us -> 0.02 us
  waiting for transfers between devices: 3.26 us -> 7.21 us
  Pallas kernels: 32.8 us -> 34.8 us
    dynamic_slice x2 -> x0, local copies, waits for them, and re-layouts: 4.72 us -> none  [the longest x1 3.27 us: local(): lax.dynamic_slice_in_dim(phase, mine, PART, 0)]
    all_to_all x1, waiting for transfers between devices: 3.26 us -> 7.21 us  [local(): got = lax.all_to_all(sent, 'row', 0, 0, tiled=True)]
    unnamed x14 -> x10, local copies, waits for them, and re-layouts: 2.21 us -> 0.02 us
    pallas_call x1, Pallas kernels: 2.44 us -> 3.75 us  [run_focal(): pl.pallas_call(focal_kernel, out_shape=jax.ShapeDtypeStruct((PAIR * 16, W...]
  transfers between devices with their start and end apart: 2 -> 2, of which waited for: 1 -> 1; matrix products, arithmetic and copies ran while one was open for 5% -> 0% of each run, Pallas kernels for 24% -> 25%
where the time goes in v7:
time: 94.1 us; the launch traced here: 93.8 us
  blocking collectives  39.9 us (42%)
  Pallas kernels  34.8 us (37%)
  starting transfers between devices  10.7 us (11%)
  waiting for transfers between devices  7.21 us (8%)
  other arithmetic  1.03 us (1%)
    all_to_all x1, blocking collectives, local(): got = lax.all_to_all(sent, ('band_lo', 'row'), 0, 0, tiled=True)  21 us
    all_to_all x1, blocking collectives, local(): parts = lax.all_to_all(parts, ('band_hi', 'band_lo'), 0, 0, tiled=True)  18.9 us
    pallas_call x1, Pallas kernels, run_forward(): pl.pallas_call(forward_kernel, out_shape=jax.ShapeDtypeStruct((16, WL * 2...  13.8 us
    pallas_call x1, Pallas kernels, run_side(): pl.pallas_call(side_kernel, grid=(HALF // CB,), out_shape=(jax.ShapeDtype...  10 us
    all_to_all x1, starting transfers between devices, local(): got = lax.all_to_all(sent, 'row', 0, 0, tiled=True)  8.62 us
    pallas_call x1, Pallas kernels, run_gradient(): pl.pallas_call(gradient_kernel, out_shape=jax.ShapeDtypeStruct((8, PART,...  7.31 us
    all_to_all x1, waiting for transfers between devices, local(): got = lax.all_to_all(sent, 'row', 0, 0, tiled=True)  7.21 us
    pallas_call x1, Pallas kernels, run_focal(): pl.pallas_call(focal_kernel, out_shape=jax.ShapeDtypeStruct((PAIR * 16, W...  3.75 us
  transfers between devices with their start and end apart: 2, of which 1 were waited for; matrix products, arithmetic and copies ran while one was open for 0% of the time, Pallas kernels for 25%

profile of v7, /device:TPU:1, one launch (start us, length us, event | category | flops | bytes accessed | tf_op | source)
XLA Modules:
  0.0 93.8 jit_solution(6813463050215274524)
XLA Ops:
  0.0 0.0 copy-start.4
  0.0 2.1 %collective-permute-start = (s32[2]{0:T(128)}, s32[2]{0:T(128)S(1)}, u32[]{:S(2)}, u32[]{:S(2)}) collective-permute-start(s32[2]{0:T(128)} %level.1), channel_id=1, source_target_pairs={{0,16},{16,0},{1,17},{17,1},{2,18},{18,2},{3,19},{19,3},{4,20},{20... | collective-permute-start | bytes 32 | tf_op jit(solution)/shard_map/ppermute | solution.py:463
  2.1 13.8 %forward.1 = bf16[16,128,256]{2,1,0:T(8,128)(2,1)} custom-call(s32[2]{0:T(128)} %level.1, f32[256,4096]{1,0:T(8,128)} %ph_l, s32[256,4096]{1,0:T(8,128)} %ap_l), custom_call_target="tpu_custom_call" | custom-call | tf_op jit(solution)/shard_map/forward/pallas_call | solution.py:377
  15.9 0.0 collective-permute-done
  15.9 0.0 copy-done.4
  15.9 0.1 pad_add_fusion.level
  16.0 8.6 %all-to-all-start = ((bf16[16,128,256]{2,1,0:T(8,128)(2,1)}), bf16[16,128,256]{2,1,0:T(8,128)(2,1)S(1)}, u32[]{:S(2)}, u32[]{:S(2)}) async-start(bf16[16,128,256]{2,1,0:T(8,128)(2,1)} %forward.1), calls=%async_computation | async-start | bytes 2097152 | tf_op jit(solution)/shard_map/all_to_all | solution.py:466
  24.6 0.0 copy-start.3
  24.6 10.0 %side.1 = (bf16[16,2,256,2048]{3,2,1,0:T(8,128)(2,1)}, bf16[2,2,256,2048]{3,2,1,0:T(8,128)(2,1)}, bf16[2,2,256,2048]{3,2,1,0:T(8,128)(2,1)}, f32[4,128,2048]{2,1,0:T(8,128)}) custom-call(f32[256,4096]{1,0:T(8,128)} %ph_l, f32[256,4096]{1,0:T(8,128)} %ph_l, s32[256,4096]{1,0:T(8,128)} %ap_l, s32[256,4096]{1,0:T(8,128)} %ap_l), custom_call_target="tpu_custom_call" | custom-call | flops 4294967296 | bytes 16777216 | tf_op jit(solution)/shard_map/side/pallas_call | solution.py:400
  34.6 7.2 %all-to-all-done.x = bf16[16,128,256]{2,1,0:T(8,128)(2,1)S(1)} async-done(((bf16[16,128,256]{2,1,0:T(8,128)(2,1)}), bf16[16,128,256]{2,1,0:T(8,128)(2,1)S(1)}, u32[]{:S(2)}, u32[]{:S(2)}) %all-to-all-start) | async-done | bytes 1048608 | tf_op jit(solution)/shard_map/all_to_all | solution.py:466
  41.8 0.0 copy-done.3
  41.8 0.0 copy-start
  41.8 0.0 copy-start.1
  41.8 0.0 copy-start.2
  41.8 3.7 %focal.1 = bf16[32,128,128]{2,1,0:T(8,128)(2,1)S(1)} custom-call(bf16[16,128,256]{2,1,0:T(8,128)(2,1)S(1)} %all-to-all-done.x, bf16[16,2,256,2048]{3,2,1,0:T(8,128)(2,1)} %get-tuple-element.27.far, f32[2,32,512]{2,1,0:T(8,128)S(1)} %copy-done.3), custom_call_target="tpu_custom_call" | custom-call | flops 17179869184 | bytes 67108864 | tf_op jit(solution)/shard_map/focal/pallas_call | solution.py:423
  45.6 21.0 %all_to_all.15.x = bf16[32,128,128]{2,1,0:T(8,128)(2,1)S(1)} all-to-all(bf16[32,128,128]{2,1,0:T(8,128)(2,1)S(1)} %focal.1), channel_id=1, replica_groups=mesh['band_hi'=4,'band_lo'=2,'row'=16] {'band_lo','row'}, dimensions={0} | all-to-all | bytes 2097152 | tf_op jit(solution)/shard_map/all_to_all | solution.py:470
  66.6 0.0 copy-done
  66.6 0.0 copy-done.1
  66.6 0.0 copy-done.2
  66.6 7.3 %gradient.1 = bf16[8,128,512]{2,1,0:T(8,128)(2,1)S(1)} custom-call(s32[4]{0:T(128)S(1)} %pad_add_fusion.level, bf16[32,128,128]{2,1,0:T(8,128)(2,1)S(1)} %all_to_all.15.x, bf16[2,2,256,2048]{3,2,1,0:T(8,128)(2,1)S(1)} %copy-done, bf16[2,2,256,2048]{3,2,1,0:T(8,128)(2,1)S(1)} %copy-done.1, f32[4,128,2048]{2,1,0:T(8,128)S(1)} %copy-done.2), custom_call_target="tpu_custom_call" | custom-call | flops 17179869184 | bytes 67108864 | tf_op jit(solution)/shard_map/gradient/pallas_call | solution.py:444
  74.0 18.9 %all_to_all.16 = bf16[8,128,512]{2,1,0:T(8,128)(2,1)S(1)} all-to-all(bf16[8,128,512]{2,1,0:T(8,128)(2,1)S(1)} %gradient.1), channel_id=1, replica_groups=mesh['band_hi'=4,'band_lo'=2,'row'=16] {'band_hi','band_lo'}, dimensions={0} | all-to-all | bytes 2097152 | tf_op jit(solution)/shard_map/all_to_all | solution.py:472
  92.8 1.0 %convert_reduce_fusion = f32[256,512]{1,0:T(8,128)} fusion(bf16[4,256,512]{2,1,0:T(8,128)(2,1)S(1)} %bitcast.4), kind=kLoop, calls=%fused_computation | loop fusion | flops 917504 | bytes 1572864 | tf_op jit(solution)/shard_map/reduce_sum | solution.py:473
Async XLA Ops:
  0.0 15.9 %copy-start.4 = (s32[2]{0:T(128)S(1)}, s32[2]{0:T(128)}, u32[]{:S(2)}) copy-start(s32[2]{0:T(128)} %level.1) | copy-start | bytes 28
  0.0 15.9 %collective-permute-start = (s32[2]{0:T(128)}, s32[2]{0:T(128)S(1)}, u32[]{:S(2)}, u32[]{:S(2)}) collective-permute-start(s32[2]{0:T(128)} %level.1), channel_id=1, source_target_pairs={{0,16},{16,0},{1,17},{17,1},{2,18},{18,2},{3,19},{19,3},{4,20},{20... | collective-permute-start | bytes 32 | tf_op jit(solution)/shard_map/ppermute | solution.py:463
  16.0 25.8 %all-to-all-start = ((bf16[16,128,256]{2,1,0:T(8,128)(2,1)}), bf16[16,128,256]{2,1,0:T(8,128)(2,1)S(1)}, u32[]{:S(2)}, u32[]{:S(2)}) async-start(bf16[16,128,256]{2,1,0:T(8,128)(2,1)} %forward.1), calls=%async_computation | async-start | bytes 2097152 | tf_op jit(solution)/shard_map/all_to_all | solution.py:466
  24.6 17.2 %copy-start.3 = (f32[2,32,512]{2,1,0:T(8,128)S(1)}, f32[2,32,512]{2,1,0:T(8,128)}, u32[]{:S(2)}) copy-start(f32[2,32,512]{2,1,0:T(8,128)} %seen.1) | copy-start | bytes 393220
  41.8 24.8 %copy-start = (bf16[2,2,256,2048]{3,2,1,0:T(8,128)(2,1)S(1)}, bf16[2,2,256,2048]{3,2,1,0:T(8,128)(2,1)}, u32[]{:S(2)}) copy-start(bf16[2,2,256,2048]{3,2,1,0:T(8,128)(2,1)} %get-tuple-element.28.tab) | copy-start | bytes 12582916
  41.8 24.8 %copy-start.1 = (bf16[2,2,256,2048]{3,2,1,0:T(8,128)(2,1)S(1)}, bf16[2,2,256,2048]{3,2,1,0:T(8,128)(2,1)}, u32[]{:S(2)}) copy-start(bf16[2,2,256,2048]{3,2,1,0:T(8,128)(2,1)} %get-tuple-element.29.tab2) | copy-start | bytes 12582916
  41.8 24.8 %copy-start.2 = (f32[4,128,2048]{2,1,0:T(8,128)S(1)}, f32[4,128,2048]{2,1,0:T(8,128)}, u32[]{:S(2)}) copy-start(f32[4,128,2048]{2,1,0:T(8,128)} %get-tuple-element.30.fld) | copy-start | bytes 12582916

commit v8 on v7

--- a/solution.py
+++ b/solution.py
@@ -21,6 +21,7 @@
 FWD_VMEM = 57
 SIDE_VMEM = 57
 FAR = 8
+WIDE = 512
 STEP = 256
 DOT = 512
 CHUNK = 32
@@ -340,24 +341,24 @@
         per = M // CB
         right = 4 + i // per, pl.multiple_of(i % per * CB, CB)
         left = 3 - i // per, pl.multiple_of((per - 1 - i % per) * CB, CB)
-        for h in range(0, CB, SUB):
-            cols = pl.ds(pl.multiple_of(base + h, SUB), SUB)
+        for h in range(0, CB, WIDE):
+            cols = pl.ds(pl.multiple_of(base + h, WIDE), WIDE)
             for w in range(PAIR * WL):
                 table = tab if w < WL else tab2
                 for n in range(2):
-                    sp[w, n, :, h : h + SUB] = nn(lhs[w, n], table[w % WL, n, :, cols])
+                    sp[w, n, :, h : h + WIDE] = nn(lhs[w, n], table[w % WL, n, :, cols])
             for r0 in range(0, PART, CHUNK):
                 sl = slice(r0, r0 + CHUNK)
                 im = slice(PART + r0, PART + r0 + CHUNK)
                 tot = [0.0, 0.0, 0.0, 0.0]
                 for w in range(PAIR * WL):
-                    dc, ds = dx[w][0][:, h : h + SUB], dx[w][1][:, h : h + SUB]
+                    dc, ds = dx[w][0][:, h : h + WIDE], dx[w][1][:, h : h + WIDE]
                     m = [
-                        jnp.concatenate([mid[w, part, sl, :]] * (SUB // 128), axis=1)
+                        jnp.concatenate([mid[w, part, sl, :]] * (WIDE // 128), axis=1)
                         for part in range(2)
                     ]
-                    cr, ci = sp[w, 0, sl, h : h + SUB] + m[0], sp[w, 0, im, h : h + SUB] + m[1]
-                    sr, si = sp[w, 1, sl, h : h + SUB], sp[w, 1, im, h : h + SUB]
+                    cr, ci = sp[w, 0, sl, h : h + WIDE] + m[0], sp[w, 0, im, h : h + WIDE] + m[1]
+                    sr, si = sp[w, 1, sl, h : h + WIDE], sp[w, 1, im, h : h + WIDE]
                     tot[0] += cr * dc + ci * ds
                     tot[1] += ci * dc - cr * ds
                     tot[2] += sr * dc + si * ds
@@ -365,8 +366,8 @@
                 cr, ci, sr, si = tot
                 g_r = (ci + sr) * fld[0, sl, cols] - (cr - si) * fld[1, sl, cols]
                 g_l = (ci - sr) * fld[2, sl, cols] - (cr + si) * fld[3, sl, cols]
-                out[right[0], sl, pl.ds(right[1] + h, SUB)] = g_r.astype(BF16)
-                out[left[0], sl, pl.ds(left[1] + (CB - SUB - h), SUB)] = lane_rev(g_l).astype(BF16)
+                out[right[0], sl, pl.ds(right[1] + h, WIDE)] = g_r.astype(BF16)
+                out[left[0], sl, pl.ds(left[1] + (CB - WIDE - h), WIDE)] = lane_rev(g_l).astype(BF16)
         return 0
 
     lax.fori_loop(0, HALF // CB, block, 0)

time: 94.1 us -> 93.9 us (level)
  no operation moved by 1% of the time
where the time goes in v8:
time: 93.9 us; the launch traced here: 93.6 us
  blocking collectives  39.9 us (42%)
  Pallas kernels  34.6 us (37%)
  starting transfers between devices  10.7 us (11%)
  waiting for transfers between devices  7.21 us (8%)
  other arithmetic  1.03 us (1%)
    all_to_all x1, blocking collectives, local(): got = lax.all_to_all(sent, ('band_lo', 'row'), 0, 0, tiled=True)  21 us
    all_to_all x1, blocking collectives, local(): parts = lax.all_to_all(parts, ('band_hi', 'band_lo'), 0, 0, tiled=True)  18.8 us
    pallas_call x1, Pallas kernels, run_forward(): pl.pallas_call(forward_kernel, out_shape=jax.ShapeDtypeStruct((16, WL * 2...  13.8 us
    pallas_call x1, Pallas kernels, run_side(): pl.pallas_call(side_kernel, grid=(HALF // CB,), out_shape=(jax.ShapeDtype...  10 us
    all_to_all x1, starting transfers between devices, local(): got = lax.all_to_all(sent, 'row', 0, 0, tiled=True)  8.62 us
    all_to_all x1, waiting for transfers between devices, local(): got = lax.all_to_all(sent, 'row', 0, 0, tiled=True)  7.21 us
    pallas_call x1, Pallas kernels, run_gradient(): pl.pallas_call(gradient_kernel, out_shape=jax.ShapeDtypeStruct((8, PART,...  7.13 us
    pallas_call x1, Pallas kernels, run_focal(): pl.pallas_call(focal_kernel, out_shape=jax.ShapeDtypeStruct((PAIR * 16, W...  3.75 us
  transfers between devices with their start and end apart: 2, of which 1 were waited for; matrix products, arithmetic and copies ran while one was open for 0% of the time, Pallas kernels for 25%

profile of v8, /device:TPU:1, one launch (start us, length us, event | category | flops | bytes accessed | tf_op | source)
XLA Modules:
  0.0 93.6 jit_solution(14220817009271888853)
XLA Ops:
  0.0 0.0 copy-start.4
  0.0 2.1 %collective-permute-start = (s32[2]{0:T(128)}, s32[2]{0:T(128)S(1)}, u32[]{:S(2)}, u32[]{:S(2)}) collective-permute-start(s32[2]{0:T(128)} %level.1), channel_id=1, source_target_pairs={{0,16},{16,0},{1,17},{17,1},{2,18},{18,2},{3,19},{19,3},{4,20},{20... | collective-permute-start | bytes 32 | tf_op jit(solution)/shard_map/ppermute | solution.py:464
  2.1 13.8 %forward.1 = bf16[16,128,256]{2,1,0:T(8,128)(2,1)} custom-call(s32[2]{0:T(128)} %level.1, f32[256,4096]{1,0:T(8,128)} %ph_l, s32[256,4096]{1,0:T(8,128)} %ap_l), custom_call_target="tpu_custom_call" | custom-call | tf_op jit(solution)/shard_map/forward/pallas_call | solution.py:378
  15.9 0.0 collective-permute-done
  15.9 0.0 copy-done.4
  15.9 0.1 pad_add_fusion.level
  16.0 8.6 %all-to-all-start = ((bf16[16,128,256]{2,1,0:T(8,128)(2,1)}), bf16[16,128,256]{2,1,0:T(8,128)(2,1)S(1)}, u32[]{:S(2)}, u32[]{:S(2)}) async-start(bf16[16,128,256]{2,1,0:T(8,128)(2,1)} %forward.1), calls=%async_computation | async-start | bytes 2097152 | tf_op jit(solution)/shard_map/all_to_all | solution.py:467
  24.6 0.0 copy-start.3
  24.6 10.0 %side.1 = (bf16[16,2,256,2048]{3,2,1,0:T(8,128)(2,1)}, bf16[2,2,256,2048]{3,2,1,0:T(8,128)(2,1)}, bf16[2,2,256,2048]{3,2,1,0:T(8,128)(2,1)}, f32[4,128,2048]{2,1,0:T(8,128)}) custom-call(f32[256,4096]{1,0:T(8,128)} %ph_l, f32[256,4096]{1,0:T(8,128)} %ph_l, s32[256,4096]{1,0:T(8,128)} %ap_l, s32[256,4096]{1,0:T(8,128)} %ap_l), custom_call_target="tpu_custom_call" | custom-call | flops 4294967296 | bytes 16777216 | tf_op jit(solution)/shard_map/side/pallas_call | solution.py:401
  34.6 7.2 %all-to-all-done.x = bf16[16,128,256]{2,1,0:T(8,128)(2,1)S(1)} async-done(((bf16[16,128,256]{2,1,0:T(8,128)(2,1)}), bf16[16,128,256]{2,1,0:T(8,128)(2,1)S(1)}, u32[]{:S(2)}, u32[]{:S(2)}) %all-to-all-start) | async-done | bytes 1048608 | tf_op jit(solution)/shard_map/all_to_all | solution.py:467
  41.8 0.0 copy-done.3
  41.8 0.0 copy-start
  41.8 0.0 copy-start.1
  41.8 0.0 copy-start.2
  41.8 3.7 %focal.1 = bf16[32,128,128]{2,1,0:T(8,128)(2,1)S(1)} custom-call(bf16[16,128,256]{2,1,0:T(8,128)(2,1)S(1)} %all-to-all-done.x, bf16[16,2,256,2048]{3,2,1,0:T(8,128)(2,1)} %get-tuple-element.27.far, f32[2,32,512]{2,1,0:T(8,128)S(1)} %copy-done.3), custom_call_target="tpu_custom_call" | custom-call | flops 17179869184 | bytes 67108864 | tf_op jit(solution)/shard_map/focal/pallas_call | solution.py:424
  45.6 21.0 %all_to_all.15.x = bf16[32,128,128]{2,1,0:T(8,128)(2,1)S(1)} all-to-all(bf16[32,128,128]{2,1,0:T(8,128)(2,1)S(1)} %focal.1), channel_id=1, replica_groups=mesh['band_hi'=4,'band_lo'=2,'row'=16] {'band_lo','row'}, dimensions={0} | all-to-all | bytes 2097152 | tf_op jit(solution)/shard_map/all_to_all | solution.py:471
  66.6 0.0 copy-done
  66.6 0.0 copy-done.1
  66.6 0.0 copy-done.2
  66.6 7.1 %gradient.1 = bf16[8,128,512]{2,1,0:T(8,128)(2,1)S(1)} custom-call(s32[4]{0:T(128)S(1)} %pad_add_fusion.level, bf16[32,128,128]{2,1,0:T(8,128)(2,1)S(1)} %all_to_all.15.x, bf16[2,2,256,2048]{3,2,1,0:T(8,128)(2,1)S(1)} %copy-done, bf16[2,2,256,2048]{3,2,1,0:T(8,128)(2,1)S(1)} %copy-done.1, f32[4,128,2048]{2,1,0:T(8,128)S(1)} %copy-done.2), custom_call_target="tpu_custom_call" | custom-call | flops 17179869184 | bytes 67108864 | tf_op jit(solution)/shard_map/gradient/pallas_call | solution.py:445
  73.8 18.8 %all_to_all.16 = bf16[8,128,512]{2,1,0:T(8,128)(2,1)S(1)} all-to-all(bf16[8,128,512]{2,1,0:T(8,128)(2,1)S(1)} %gradient.1), channel_id=1, replica_groups=mesh['band_hi'=4,'band_lo'=2,'row'=16] {'band_hi','band_lo'}, dimensions={0} | all-to-all | bytes 2097152 | tf_op jit(solution)/shard_map/all_to_all | solution.py:473
  92.6 1.0 %convert_reduce_fusion = f32[256,512]{1,0:T(8,128)} fusion(bf16[4,256,512]{2,1,0:T(8,128)(2,1)S(1)} %bitcast.4), kind=kLoop, calls=%fused_computation | loop fusion | flops 917504 | bytes 1572864 | tf_op jit(solution)/shard_map/reduce_sum | solution.py:474
Async XLA Ops:
  0.0 15.9 %copy-start.4 = (s32[2]{0:T(128)S(1)}, s32[2]{0:T(128)}, u32[]{:S(2)}) copy-start(s32[2]{0:T(128)} %level.1) | copy-start | bytes 28
  0.0 15.9 %collective-permute-start = (s32[2]{0:T(128)}, s32[2]{0:T(128)S(1)}, u32[]{:S(2)}, u32[]{:S(2)}) collective-permute-start(s32[2]{0:T(128)} %level.1), channel_id=1, source_target_pairs={{0,16},{16,0},{1,17},{17,1},{2,18},{18,2},{3,19},{19,3},{4,20},{20... | collective-permute-start | bytes 32 | tf_op jit(solution)/shard_map/ppermute | solution.py:464
  16.0 25.8 %all-to-all-start = ((bf16[16,128,256]{2,1,0:T(8,128)(2,1)}), bf16[16,128,256]{2,1,0:T(8,128)(2,1)S(1)}, u32[]{:S(2)}, u32[]{:S(2)}) async-start(bf16[16,128,256]{2,1,0:T(8,128)(2,1)} %forward.1), calls=%async_computation | async-start | bytes 2097152 | tf_op jit(solution)/shard_map/all_to_all | solution.py:467
  24.6 17.2 %copy-start.3 = (f32[2,32,512]{2,1,0:T(8,128)S(1)}, f32[2,32,512]{2,1,0:T(8,128)}, u32[]{:S(2)}) copy-start(f32[2,32,512]{2,1,0:T(8,128)} %seen.1) | copy-start | bytes 393220
  41.8 24.8 %copy-start = (bf16[2,2,256,2048]{3,2,1,0:T(8,128)(2,1)S(1)}, bf16[2,2,256,2048]{3,2,1,0:T(8,128)(2,1)}, u32[]{:S(2)}) copy-start(bf16[2,2,256,2048]{3,2,1,0:T(8,128)(2,1)} %get-tuple-element.28.tab) | copy-start | bytes 12582916
  41.8 24.8 %copy-start.1 = (bf16[2,2,256,2048]{3,2,1,0:T(8,128)(2,1)S(1)}, bf16[2,2,256,2048]{3,2,1,0:T(8,128)(2,1)}, u32[]{:S(2)}) copy-start(bf16[2,2,256,2048]{3,2,1,0:T(8,128)(2,1)} %get-tuple-element.29.tab2) | copy-start | bytes 12582916
  41.8 24.8 %copy-start.2 = (f32[4,128,2048]{2,1,0:T(8,128)S(1)}, f32[4,128,2048]{2,1,0:T(8,128)}, u32[]{:S(2)}) copy-start(f32[4,128,2048]{2,1,0:T(8,128)} %get-tuple-element.30.fld) | copy-start | bytes 12582916
